TPU v7x, 256 devices: a whole 4x4x8 slice. The times are simulated.
256 devices in a mesh: dof: 32 (over z, x), dir: 8 (over y, core).
Axes of the slice: x: 4, y: 4, z: 8, core: 2. Of those that a mesh axis runs over, the one named last changes fastest.
Arguments:
- start_disp: float32 [4, 256, 32768], P(None, 'dir', 'dof')
- start_vel: float32 [4, 256, 32768], P(None, 'dir', 'dof')
- elem_stiff: float32 [8, 8, 32768], P(None, None, 'dof'), may hold values from -1.5 to 1.5
- link_stiff: float32 [4, 4, 32768], P(None, None, 'dof'), may hold values from -1.5 to 1.5
- block_inv: float32 [4, 4, 32768], P(None, None, 'dof'), may hold values from -0.3 to 1.4
- link_offset: int32 [32768], P('dof'), may hold values from -8 to 8
- damper_nodes: int32 [64], P('dof'), may hold values from 0 to 32767, as said below
- damper_stiff: float32 [2, 2, 64], P(None, None, 'dof'), may hold values from -4 to 4
- damper_damp: float32 [2, 2, 64], P(None, None, 'dof'), may hold values from -4 to 4
Outputs:
- end_velocity: float32 [4, 256, 32768], P(None, 'dir', 'dof')
- q_block: float32 [4, 256, 32768], P(None, None, ('dof', 'dir'))
- r_factor: float32 [256, 256], replicated
Inputs may be any that keep to these rules, and one draw needn't show every extreme that they name: `damper_nodes`: the ids rise; the k-th aligned block of 2 ids names nodes of k * 1024 to (k + 1) * 1024 - 1, its j-th id lying in j * 512 to (j + 1) * 512 - 1 of that range; nodes 0 and 32767 carry dampers.
All inputs are finite; a program needn't handle non-finite values.
Results may differ from a plain program's by a relative error of at most 0.0002.
Values sent between devices are 32-bit elements; how exact they have to be, the bound alone decides.
A program may use at most 128 MiB of HBM per device.

v0:
```python
import jax
import jax.numpy as jnp
from jax import lax
from jax.sharding import PartitionSpec as P

HALO = 8


time_step = 0.5


def padded_2(x, sides, width):
    for axis, dim in sides:
        peers, length = (lax.axis_size(axis), x.shape[dim])
        up = [(i, (i + 1) % peers) for i in range(peers - 1)]
        down = [(j, i) for i, j in up]
        last = lax.slice_in_dim(x, length - width, length, axis=dim)
        initial = lax.slice_in_dim(x, 0, width, axis=dim)
        before = lax.ppermute(last, axis, up)
        after = lax.ppermute(initial, axis, down)
        x = jnp.concatenate([before, x, after], axis=dim)
    return x


def passed_along(x, axis, by):
    peers = lax.axis_size(axis)
    pairs = [(i, i + by) for i in range(peers) if 0 <= i + by < peers]
    return lax.ppermute(x, axis, pairs)


def apply_block(block, field):
    summed = block[:, 0, None, :] * field[0][None]
    for column in range(1, block.shape[1]):
        summed = summed + block[:, column, None, :] * field[column][None]
    return summed


def forces(
    disp, veloc, elem_stiff, link_stiff, block_inv, partner, damp_local, damper_stiff, damper_damp
):
    node_count = disp.shape[2]
    padded = padded_2(disp, (("dof", 2),), HALO)
    ahead_disp = padded[:, :, HALO + 1 : HALO + 1 + node_count]
    stacked = jnp.concatenate([disp, ahead_disp], axis=0)
    own_part = apply_block(elem_stiff[0:4], stacked)
    next_part = apply_block(elem_stiff[4:8], stacked)
    carried = passed_along(next_part[:, :, node_count - 1 :], "dof", 1)
    behind = jnp.concatenate([carried, next_part[:, :, : node_count - 1]], axis=2)
    linked = jnp.take(padded, partner, axis=2)
    summed = own_part + behind + apply_block(link_stiff, linked)
    lateral_disp = disp[0:2][:, :, damp_local]
    lateral_vel = veloc[0:2][:, :, damp_local]
    film_force = apply_block(damper_stiff, lateral_disp) + apply_block(damper_damp, lateral_vel)
    summed = summed.at[0:2, :, damp_local].add(film_force)
    return apply_block(block_inv, -summed)


def on_device(
    start_disp,
    start_vel,
    elem_stiff,
    link_stiff,
    block_inv,
    link_offset,
    damper_nodes,
    damper_stiff,
    damper_damp,
):
    node_count = start_disp.shape[2]
    positions = jnp.arange(node_count, dtype=jnp.int32)
    partner = HALO + positions + link_offset
    damp_local = damper_nodes - lax.axis_index("dof") * node_count
    disp = start_disp
    veloc = start_vel
    accel = forces(
        disp,
        veloc,
        elem_stiff,
        link_stiff,
        block_inv,
        partner,
        damp_local,
        damper_stiff,
        damper_damp,
    )
    for repeat in range(2):
        disp = disp + time_step * veloc + 0.5 * time_step * time_step * accel
        middle = veloc + 0.5 * time_step * accel
        accel = forces(
            disp,
            middle,
            elem_stiff,
            link_stiff,
            block_inv,
            partner,
            damp_local,
            damper_stiff,
            damper_damp,
        )
        veloc = middle + 0.5 * time_step * accel
    rows_total = 4.0 * node_count * lax.axis_size("dof")
    row_part = lax.all_to_all(disp, "dir", split_axis=2, concat_axis=1, tiled=True)
    gram_local = jnp.einsum("cdn,cen->de", row_part, row_part, precision=lax.Precision.HIGHEST)
    gram_matrix = lax.psum(gram_local, ("dof", "dir"))
    lower_factor = jnp.linalg.cholesky(gram_matrix / rows_total)
    q_parts = []
    for component in range(4):
        q_parts.append(
            lax.linalg.triangular_solve(
                lower_factor, row_part[component], left_side=True, lower=True
            )
        )
    q_block = jnp.stack(q_parts, axis=0)
    return (veloc, q_block, jnp.transpose(lower_factor))


def solution(mesh):
    in_specs = (
        P(None, "dir", "dof"),
        P(None, "dir", "dof"),
        P(None, None, "dof"),
        P(None, None, "dof"),
        P(None, None, "dof"),
        P("dof"),
        P("dof"),
        P(None, None, "dof"),
        P(None, None, "dof"),
    )
    out_specs = (P(None, "dir", "dof"), P(None, None, ("dof", "dir")), P())
    return jax.shard_map(
        on_device, mesh=mesh, in_specs=in_specs, out_specs=out_specs, check_vma=False
    )
```

profile of v0, /device:TPU:1, one launch (start us, length us, event | category | flops | bytes accessed | tf_op | source)
XLA Modules:
  0.0 622.7 jit_solution(9965133149042987513)
XLA Ops:
  10.1 5.3 collective-permute-start.2
  15.5 1.9 constant_dynamic-update-slice_fusion.1
  52.1 3.5 collective-permute-start.1
  58.7 5.6 gather_fusion.6
  64.4 3.9 select_bitcast_fusion.2
  68.3 2.2 fusion.42
  70.5 1.9 copy.217
  73.6 2.7 fusion
  78.1 12.0 %while.11 = (s32[]{:T(128)}, f32[4,32,1024]{1,0,2:T(4,128)S(1)}, s32[2,2]{1,0:T(2,128)S(1)}, f32[2,2,32]{2,1,0:T(2,128)S(1)}, s32[]{:T(128)}, /*index=5*/s32[3]{0:T(128)S(1)}, s32[1]{0:T(128)}, s32[]{:T(128)}) while((s32[]{:T(128)}, f32[4,32,1024]{1,0,2:T(4,128)S(1)}, s32[2,2]{1,0:T(2,128)S(1)}, f32[2,2,32]{2,1,0:T(2,128)S(1)}, s32[]{:T(128)}, ...), condition=%wide.while_cond.1, body=%wide.while_body.1.sunk | while | flops 147 | bytes 1443 | solution.py:54
  78.7 2.0 and_reduce_fusion.6
  80.7 1.9 add_select_fusion.6
  84.7 2.0 and_reduce_fusion.6
  86.7 1.9 add_select_fusion.6
  93.4 6.8 %multiply_add_fusion.3 = (f32[4,32,1024]{1,0,2:T(4,128)S(1)}, f32[4,32,1024]{1,0,2:T(4,128)}) fusion(f32[4,32,1024]{1,0,2:T(4,128)S(1)} %copy-done.6, f32[4,32,1024]{1,0,2:T(4,128)S(1)} %copy-done.7, f32[32,1024]{0,1:T(8,128)S(1)} %bitcast.297, f32[4,1024]{0,1:T(8,128)S(1)} %bitcast.287, f32[32,1024]{0,1:T(8,128)S(1)} %bitcast.298, ...), kind=kLoop, calls=%fused_computation.28 | loop fusion | flops 1572864 | bytes 3211264 | tf_op jit(solution)/shard_map/add | solution.py:87
  102.2 2.7 fusion.40
  104.9 1.9 gather_fusion.2
  106.9 2.9 slice.759
  109.8 1.9 gather_fusion.3
  113.0 4.8 collective-permute-start.5
  123.6 1.9 copy.239
  125.5 3.1 pad_maximum_fusion
  128.6 9.6 %gather_fusion.7 = f32[1024,4,32]{2,1,0:T(4,128)} fusion(f32[4,32,1040]{1,0,2:T(4,128)} %pad_maximum_fusion, s32[1024]{0:T(1024)} %fusion.28), kind=kCustom, calls=%fused_computation.1.clone | custom fusion | bytes 1052672 | tf_op jit(solution)/shard_map/jit(_take)/gather | solution.py:49
  138.2 5.2 select_bitcast_fusion.1
  143.4 2.8 fusion.38
  151.9 4.1 collective-permute-start.4
  163.5 2.9 fusion.1
  166.4 2.6 copy.246
  169.0 16.8 %while.12 = (s32[]{:T(128)}, f32[4,32,1024]{1,0,2:T(4,128)}, s32[2,2]{1,0:T(2,128)}, f32[2,2,32]{2,1,0:T(2,128)S(1)}, s32[]{:T(128)}, /*index=5*/s32[3]{0:T(128)S(1)}, s32[1]{0:T(128)}, s32[]{:T(128)}) while((s32[]{:T(128)}, f32[4,32,1024]{1,0,2:T(4,128)}, s32[2,2]{1,0:T(2,128)}, f32[2,2,32]{2,1,0:T(2,128)S(1)}, s32[]{:T(128)}, ...), condition=%wide.while_cond.2, body=%wide.while_body.2.sunk | while | flops 147 | bytes 1443 | solution.py:54
  170.2 2.0 and_reduce_fusion.7
  172.2 2.6 add_select_fusion.7
  174.9 2.6 dynamic-update-slice.30
  178.7 2.0 and_reduce_fusion.7
  180.7 2.6 add_select_fusion.7
  183.3 2.6 dynamic-update-slice.30
  185.9 2.0 neg.10
  189.8 6.5 %multiply_add_fusion.1 = (f32[4,32,1024]{1,0,2:T(4,128)S(1)}, f32[4,32,1024]{1,0,2:T(4,128)}) fusion(f32[4,32,1024]{1,0,2:T(4,128)S(1)} %get-tuple-element.161, f32[4,32,1024]{1,0,2:T(4,128)S(1)} %copy-done.2, f32[32,1024]{0,1:T(8,128)S(1)} %bitcast.305, f32[32,1024]{0,1:T(8,128)S(1)} %bitcast.306, f32[32,1024]{0,1:T(8,128)S(1)} %bitcast.307, ...), kind=kLoop, calls=%fused_computation.26 | loop fusion | flops 1835008 | bytes 2686976 | tf_op jit(solution)/shard_map/add | solution.py:87
  198.5 2.8 fusion.36
  201.3 3.5 reshape.246
  204.8 6.7 %all-to-all-start = ((f32[8,1,16384]{2,1,0:T(1,128)}), f32[8,1,16384]{2,1,0:T(1,128)}, u32[]{:S(2)}, u32[]{:S(2)}) async-start(f32[8,1,16384]{2,1,0:T(1,128)} %reshape.246), calls=%async_computation | async-start | bytes 1048576 | tf_op jit(solution)/shard_map/all_to_all | solution.py:102
  211.5 1.9 gather_fusion.4
  213.4 2.9 slice.781
  216.4 1.9 gather_fusion.5
  219.6 5.0 collective-permute-start.8
  232.3 3.1 pad_maximum_fusion.1
  235.4 5.6 gather_fusion.8
  241.0 3.9 select_bitcast_fusion
  244.9 2.2 fusion.34
  252.2 3.5 collective-permute-start.7
  258.7 2.6 fusion.2
  263.2 12.0 %while.13 = (s32[]{:T(128)}, f32[4,32,1024]{1,0,2:T(4,128)S(1)}, s32[2,2]{1,0:T(2,128)S(1)}, f32[2,2,32]{2,1,0:T(2,128)S(1)}, s32[]{:T(128)}, /*index=5*/s32[3]{0:T(128)S(1)}, s32[1]{0:T(128)}, s32[]{:T(128)}) while((s32[]{:T(128)}, f32[4,32,1024]{1,0,2:T(4,128)S(1)}, s32[2,2]{1,0:T(2,128)S(1)}, f32[2,2,32]{2,1,0:T(2,128)S(1)}, s32[]{:T(128)}, ...), condition=%wide.while_cond.3, body=%wide.while_body.3.sunk | while | flops 147 | bytes 1443 | solution.py:54
  263.8 2.0 and_reduce_fusion.8
  265.8 1.9 add_select_fusion.8
  269.8 2.0 and_reduce_fusion.8
  271.8 1.9 add_select_fusion.8
  277.5 5.9 multiply_add_fusion
  285.4 2.9 reduce.18
  291.7 254.4 %all-reduce.4.cloned.1.call-done = f32[256,256]{0,1:T(8,128)} async-done(((f32[256,256]{0,1:T(8,128)}), f32[256,256]{0,1:T(8,128)}) %all-reduce.4.cloned.1.call-update) | async-done | bytes 262160 | tf_op jit(solution)/shard_map/psum | solution.py:104
  548.3 11.7 %cholesky.50 = f32[128,128]{1,0:T(8,128)S(1)} custom-call(f32[128,128]{1,0:T(8,128)S(1)} %cholesky.118), custom_call_target="Cholesky" | custom-call | tf_op jit(solution)/shard_map/jit(cholesky)/cholesky | solution.py:105
  560.1 9.8 %custom-call.14 = f32[1,128,128]{1,2,0:T(8,128)S(1)} custom-call(f32[1,128,128]{2,1,0:T(8,128)S(1)} %get-tuple-element.242), custom_call_target="InvertDiagBlocksLowerTriangular" | custom-call | tf_op jit(solution)/shard_map/jit(cholesky)/cholesky | solution.py:105
  570.4 11.7 %cholesky.105 = f32[128,128]{1,0:T(8,128)S(1)} custom-call(f32[128,128]{1,0:T(8,128)S(1)} %convolution_subtract_fusion.4), custom_call_target="Cholesky" | custom-call | tf_op jit(solution)/shard_map/jit(cholesky)/cholesky | solution.py:105
  584.8 5.2 while.14
  585.4 2.0 bitcast_dynamic-update-slice_fusion.2
  588.0 2.0 bitcast_dynamic-update-slice_fusion.2
  590.0 20.7 %custom-call.18 = f32[2,128,128]{1,2,0:T(8,128)S(1)} custom-call(f32[2,128,128]{2,1,0:T(8,128)} %get-tuple-element.55), custom_call_target="InvertDiagBlocksLowerTriangular" | custom-call | tf_op jit(solution)/shard_map/triangular_solve/custom-call.0 | solution.py:109
  (298 shorter events, 119.8 us)
Async XLA Ops:
  7.2 11.4 %copy-start.55 = (s32[1024]{0:T(1024)S(1)}, s32[1024]{0:T(1024)}, u32[]{:S(2)}) copy-start(s32[1024]{0:T(1024)} %param.18) | copy-start | bytes 12292
  7.2 12.6 %copy-start.60 = (s32[2]{0:T(128)S(1)}, s32[2]{0:T(128)}, u32[]{:S(2)}) copy-start(s32[2]{0:T(128)} %param.19) | copy-start | bytes 28
  7.2 13.1 %copy-start.14 = (f32[4,32,1024]{2,1,0:T(8,128)S(1)}, f32[4,32,1024]{2,1,0:T(8,128)}, u32[]{:S(2)}) copy-start(f32[4,32,1024]{2,1,0:T(8,128)} %param.14) | copy-start | bytes 1572868
  8.8 40.1 %collective-permute-start = (f32[4,32,8]{2,1,0:T(8,128)}, f32[4,32,8]{2,1,0:T(8,128)}, u32[]{:S(2)}, u32[]{:S(2)}) collective-permute-start(f32[4,32,8]{2,1,0:T(8,128)} %get-tuple-element.216), channel_id=1, source_target_pairs={{8,0},{16,8},{24,16},{32,24},{40,32},{48,40},{56,48},{64,56},{72,6... | collective-permute-start | bytes 12296 | tf_op jit(solution)/shard_map/ppermute | solution.py:20
  10.1 10.2 %copy-start.33 = (f32[8,8,1024]{2,1,0:T(8,128)S(1)}, f32[8,8,1024]{2,1,0:T(8,128)}, u32[]{:S(2)}) copy-start(f32[8,8,1024]{2,1,0:T(8,128)} %param.15) | copy-start | bytes 786436
  10.1 45.5 %collective-permute-start.2 = (f32[4,32,8]{2,1,0:T(8,128)}, f32[4,32,8]{2,1,0:T(8,128)}, u32[]{:S(2)}, u32[]{:S(2)}) collective-permute-start(f32[4,32,8]{2,1,0:T(8,128)} %get-tuple-element.215), channel_id=1, source_target_pairs={{0,8},{8,16},{16,24},{24,32},{32,40},{40,48},{48,56},{56,64},{64,7... | collective-permute-start | bytes 12296 | tf_op jit(solution)/shard_map/ppermute | solution.py:19
  17.4 3.8 copy-start.38
  17.4 4.5 slice-start
  18.6 31.5 %copy-start.28 = (f32[32,1024]{1,0:T(8,128)}, f32[32,1024]{1,0:T(8,128)S(1)}, u32[]{:S(2)}) copy-start(f32[32,1024]{1,0:T(8,128)S(1)} %get-tuple-element.220) | copy-start | bytes 393220
  18.6 4.9 slice-start.1
  20.3 4.4 copy-start.57
  20.3 5.5 copy-start.39
  21.9 2.8 copy-start.56
  24.1 18.1 %copy-start.4 = (f32[4,32,1024]{2,1,0:T(8,128)S(1)}, f32[4,32,1024]{2,1,0:T(8,128)}, u32[]{:S(2)}) copy-start(f32[4,32,1024]{2,1,0:T(8,128)} %param.13) | copy-start | bytes 1572868
  24.8 19.1 %copy-start.43 = (f32[2,2]{0,1:T(2,128)}, f32[2,2]{0,1:T(2,128)S(1)}, u32[]{:S(2)}) copy-start(f32[2,2]{0,1:T(2,128)S(1)} %copy.221) | copy-start | bytes 52
  24.9 19.0 %copy-start.46 = (f32[2,2]{0,1:T(2,128)}, f32[2,2]{0,1:T(2,128)S(1)}, u32[]{:S(2)}) copy-start(f32[2,2]{0,1:T(2,128)S(1)} %copy.223) | copy-start | bytes 52
  25.7 18.2 %copy-start.49 = (f32[2,2]{0,1:T(2,128)}, f32[2,2]{0,1:T(2,128)S(1)}, u32[]{:S(2)}) copy-start(f32[2,2]{0,1:T(2,128)S(1)} %copy.224) | copy-start | bytes 52
  25.8 18.1 %copy-start.52 = (f32[2,2]{0,1:T(2,128)}, f32[2,2]{0,1:T(2,128)S(1)}, u32[]{:S(2)}) copy-start(f32[2,2]{0,1:T(2,128)S(1)} %copy.226) | copy-start | bytes 52
  40.5 3.5 copy-start.62
  44.9 4.1 copy-start.19
  50.0 5.6 copy-start.30
  50.0 5.6 copy-start.31
  50.0 5.6 copy-start.32
  50.0 6.8 %copy-start.29 = (f32[32,1024]{1,0:T(8,128)}, f32[32,1024]{1,0:T(8,128)S(1)}, u32[]{:S(2)}) copy-start(f32[32,1024]{1,0:T(8,128)S(1)} %get-tuple-element.207) | copy-start | bytes 393220
  51.3 5.6 copy-start.15
  52.1 21.5 %collective-permute-start.1 = (f32[4,32,1]{2,1,0:T(8,128)}, f32[4,32,1]{2,1,0:T(8,128)}, u32[]{:S(2)}, u32[]{:S(2)}) collective-permute-start(f32[4,32,1]{2,1,0:T(8,128)} %slice.730), channel_id=1, source_target_pairs={{0,8},{8,16},{16,24},{24,32},{32,40},{40,48},{48,56},{56,64},{64,7... | collective-permute-start | bytes 1544 | tf_op jit(solution)/shard_map/ppermute | solution.py:28
  70.5 3.1 copy-start.16
  90.1 2.1 copy-start.7
  90.1 2.1 copy-start.8
  90.1 2.1 copy-start.11
  90.6 2.2 copy-start.5
  90.6 2.8 copy-start.6
  104.9 12.9 %copy-start.44 = (f32[2,2]{0,1:T(2,128)S(1)}, f32[2,2]{0,1:T(2,128)}, u32[]{:S(2)}) copy-start(f32[2,2]{0,1:T(2,128)} %copy-done.43) | copy-start | bytes 52
  104.9 12.9 %copy-start.47 = (f32[2,2]{0,1:T(2,128)S(1)}, f32[2,2]{0,1:T(2,128)}, u32[]{:S(2)}) copy-start(f32[2,2]{0,1:T(2,128)} %copy-done.46) | copy-start | bytes 52
  104.9 12.9 %copy-start.50 = (f32[2,2]{0,1:T(2,128)S(1)}, f32[2,2]{0,1:T(2,128)}, u32[]{:S(2)}) copy-start(f32[2,2]{0,1:T(2,128)} %copy-done.49) | copy-start | bytes 52
  104.9 12.9 %copy-start.53 = (f32[2,2]{0,1:T(2,128)S(1)}, f32[2,2]{0,1:T(2,128)}, u32[]{:S(2)}) copy-start(f32[2,2]{0,1:T(2,128)} %copy-done.52) | copy-start | bytes 52
  111.7 13.8 %collective-permute-start.3 = (f32[4,32,8]{1,0,2:T(4,128)}, f32[4,32,8]{1,0,2:T(4,128)}, u32[]{:S(2)}, u32[]{:S(2)}) collective-permute-start(f32[4,32,8]{1,0,2:T(4,128)} %get-tuple-element.186), channel_id=1, source_target_pairs={{8,0},{16,8},{24,16},{32,24},{40,32},{48,40},{56,48},{64,56},{72,6... | collective-permute-start | bytes 12296 | tf_op jit(solution)/shard_map/ppermute | solution.py:20
  113.0 12.5 %collective-permute-start.5 = (f32[4,32,8]{1,0,2:T(4,128)}, f32[4,32,8]{1,0,2:T(4,128)}, u32[]{:S(2)}, u32[]{:S(2)}) collective-permute-start(f32[4,32,8]{1,0,2:T(4,128)} %get-tuple-element.185), channel_id=1, source_target_pairs={{0,8},{8,16},{16,24},{24,32},{32,40},{40,48},{48,56},{56,64},{64,7... | collective-permute-start | bytes 12296 | tf_op jit(solution)/shard_map/ppermute | solution.py:19
  148.9 3.0 copy-start.24
  148.9 7.1 %copy-start.25 = (f32[32,1024]{1,0:T(8,128)}, f32[32,1024]{1,0:T(8,128)S(1)}, u32[]{:S(2)}) copy-start(f32[32,1024]{1,0:T(8,128)S(1)} %get-tuple-element.204) | copy-start | bytes 393220
  148.9 7.1 %copy-start.26 = (f32[32,1024]{1,0:T(8,128)}, f32[32,1024]{1,0:T(8,128)S(1)}, u32[]{:S(2)}) copy-start(f32[32,1024]{1,0:T(8,128)S(1)} %get-tuple-element.205) | copy-start | bytes 393220
  148.9 7.1 %copy-start.27 = (f32[32,1024]{1,0:T(8,128)}, f32[32,1024]{1,0:T(8,128)S(1)}, u32[]{:S(2)}) copy-start(f32[32,1024]{1,0:T(8,128)S(1)} %get-tuple-element.206) | copy-start | bytes 393220
  151.9 11.6 %collective-permute-start.4 = (f32[4,32,1]{2,1,0:T(8,128)}, f32[4,32,1]{2,1,0:T(8,128)}, u32[]{:S(2)}, u32[]{:S(2)}) collective-permute-start(f32[4,32,1]{2,1,0:T(8,128)} %slice.749), channel_id=1, source_target_pairs={{0,8},{8,16},{16,24},{24,32},{32,40},{40,48},{48,56},{56,64},{64,7... | collective-permute-start | bytes 1544 | tf_op jit(solution)/shard_map/ppermute | solution.py:28
  166.4 2.6 copy-start.35
  166.4 2.6 copy-start.42
  185.9 2.0 copy-start.36
  187.9 1.8 copy-start.12
  196.3 5.0 copy-start
  204.8 19.8 %copy-start.45 = (f32[2,2]{0,1:T(2,128)S(1)}, f32[2,2]{0,1:T(2,128)}, u32[]{:S(2)}) copy-start(f32[2,2]{0,1:T(2,128)} %copy-done.43) | copy-start | bytes 52
  204.8 19.8 %copy-start.48 = (f32[2,2]{0,1:T(2,128)S(1)}, f32[2,2]{0,1:T(2,128)}, u32[]{:S(2)}) copy-start(f32[2,2]{0,1:T(2,128)} %copy-done.46) | copy-start | bytes 52
  204.8 19.8 %copy-start.51 = (f32[2,2]{0,1:T(2,128)S(1)}, f32[2,2]{0,1:T(2,128)}, u32[]{:S(2)}) copy-start(f32[2,2]{0,1:T(2,128)} %copy-done.49) | copy-start | bytes 52
  204.8 19.8 %copy-start.54 = (f32[2,2]{0,1:T(2,128)S(1)}, f32[2,2]{0,1:T(2,128)}, u32[]{:S(2)}) copy-start(f32[2,2]{0,1:T(2,128)} %copy-done.52) | copy-start | bytes 52
  204.8 20.5 %copy-start.1 = (f32[4,32,1024]{1,0,2:T(4,128)S(1)}, f32[4,32,1024]{1,0,2:T(4,128)}, u32[]{:S(2)}) copy-start(f32[4,32,1024]{1,0,2:T(4,128)} %copy-done) | copy-start | bytes 1572868
  204.8 80.0 %all-to-all-start = ((f32[8,1,16384]{2,1,0:T(1,128)}), f32[8,1,16384]{2,1,0:T(1,128)}, u32[]{:S(2)}, u32[]{:S(2)}) async-start(f32[8,1,16384]{2,1,0:T(1,128)} %reshape.246), calls=%async_computation | async-start | bytes 1048576 | tf_op jit(solution)/shard_map/all_to_all | solution.py:102
  211.5 334.7 %all-reduce.4.cloned.1.call-start = ((), (), s32[]{:S(2)}) async-start(), calls=%async_computation.1 | async-start | bytes 524288 | tf_op jit(solution)/shard_map/psum | solution.py:104
  218.3 14.0 %collective-permute-start.6 = (f32[4,32,8]{1,0,2:T(4,128)}, f32[4,32,8]{1,0,2:T(4,128)}, u32[]{:S(2)}, u32[]{:S(2)}) collective-permute-start(f32[4,32,8]{1,0,2:T(4,128)} %get-tuple-element.172), channel_id=1, source_target_pairs={{8,0},{16,8},{24,16},{32,24},{40,32},{48,40},{56,48},{64,56},{72,6... | collective-permute-start | bytes 12296 | tf_op jit(solution)/shard_map/ppermute | solution.py:20
  219.6 12.7 %collective-permute-start.8 = (f32[4,32,8]{1,0,2:T(4,128)}, f32[4,32,8]{1,0,2:T(4,128)}, u32[]{:S(2)}, u32[]{:S(2)}) collective-permute-start(f32[4,32,8]{1,0,2:T(4,128)} %get-tuple-element.171), channel_id=1, source_target_pairs={{0,8},{8,16},{16,24},{24,32},{32,40},{40,48},{48,56},{56,64},{64,7... | collective-permute-start | bytes 12296 | tf_op jit(solution)/shard_map/ppermute | solution.py:19
  244.9 3.7 copy-start.18
  249.6 1.9 copy-start.21
  249.6 2.6 copy-start.22
  249.6 6.1 copy-start.23
  252.2 6.5 %collective-permute-start.7 = (f32[4,32,1]{2,1,0:T(8,128)}, f32[4,32,1]{2,1,0:T(8,128)}, u32[]{:S(2)}, u32[]{:S(2)}) collective-permute-start(f32[4,32,1]{2,1,0:T(8,128)} %slice.771), channel_id=1, source_target_pairs={{0,8},{8,16},{16,24},{24,32},{32,40},{40,48},{48,56},{56,64},{64,7... | collective-permute-start | bytes 1544 | tf_op jit(solution)/shard_map/ppermute | solution.py:28
  275.7 1.8 copy-start.13
  291.7 293.0 %copy-start.61 = (s32[2]{0:T(128)S(1)}, s32[2]{0:T(128)}, u32[]{:S(2)}) copy-start(s32[2]{0:T(128)} %iota_multiply_fusion) | copy-start | bytes 28
  (12 other events, 18.7 us)
Sparse Core Ops, SparseCore 0:
  291.8 254.3 all-reduce.3
where the time goes:
time: 630 us; the launch traced here: 623 us
  waiting for transfers between devices  254 us (40%)
  local copies, waits for them, and re-layouts  163 us (26%)
  other arithmetic  147 us (23%)
  starting transfers between devices  36.7 us (6%)
  between operations  16.7 us (3%)
    psum x1, waiting for transfers between devices, on_device(): gram_matrix = lax.psum(gram_local, ('dof', 'dir'))  254 us
    another operation x7, other arithmetic, on_device(): lower_factor = jnp.linalg.cholesky(gram_matrix / rows_total)  34.6 us
    unnamed x147, local copies, waits for them, and re-layouts  34.5 us
    scatter-add x12, other arithmetic  25.1 us
    another operation x3, other arithmetic, on_device(): lax.linalg.triangular_solve(lower_factor, row_part[component], left_side=...  21.3 us
    gather x3, local copies, waits for them, and re-layouts, forces(): linked = jnp.take(padded, partner, axis=2)  20.9 us
    slice x19, local copies, waits for them, and re-layouts, apply_block(): summed = block[:, 0, None, :] * field[0][None]  20.3 us
    mul x21, local copies, waits for them, and re-layouts, apply_block(): summed = summed + block[:, column, None, :] * field[column][None]  19.3 us
  transfers between devices with their start and end apart: 11, of which 1 were waited for; matrix products, arithmetic and copies ran while one was open for 21% of the time, Pallas kernels for 0%

commit v1 on v0

v1 whole, which is shorter than its diff:
```python
import functools

import jax
import jax.numpy as jnp
from jax import lax
from jax.experimental import pallas as pl
from jax.experimental.pallas import tpu as pltpu
from jax.sharding import PartitionSpec as P

STEP = 0.5
LANES = 128
SUB = 8
REACH = 32
MESH = pl.DeviceIdType.MESH
HIGHEST = lax.Precision.HIGHEST


def iota(shape, axis):
    return lax.broadcasted_iota(jnp.int32, shape, axis)


def rolled(x, by, axis):
    by = by % x.shape[axis]
    return pltpu.roll(x, by, axis) if by else x


def lane_gather(x, index):
    return jnp.take_along_axis(x, index, axis=1, mode="promise_in_bounds")


def newmark_kernel(
    ndof,
    ndir,
    disp_in,
    vel_in,
    elem_in,
    link_in,
    inv_in,
    offset_in,
    damper_at,
    damper_k,
    damper_c,
    vel_out,
    x_out,
    gram_out,
    disp_a,
    disp_b,
    vel,
    coef,
    link_raw,
    inv_raw,
    offset_raw,
    pm,
    qm,
    vm,
    to_send,
    arrived,
    x_all,
    gram_part,
    dir_slots,
    dir_sum,
    dof_slots,
    gram,
    load_sem,
    halo_send,
    halo_recv,
    a2a_send,
    a2a_recv,
    rs_send,
    rs_recv,
    ds_send,
    ds_recv,
    dg_send,
    dg_recv,
    ag_send,
    ag_recv,
    store_sem,
):
    me_p = lax.axis_index("dof")
    me_t = lax.axis_index("dir")
    dirs = disp_in.shape[1]
    nodes = disp_in.shape[2]
    tiles = nodes // LANES
    around = tiles + 1
    per_dof = dirs // ndof

    loads = [
        (disp_in, disp_a.at[:, :, 0:nodes]),
        (vel_in, vel.at[:, :, 0:nodes]),
        (elem_in, coef.at[0:8, :, 0:nodes]),
        (link_in, link_raw),
        (inv_in, inv_raw),
        (offset_in, offset_raw),
    ]
    loads = [pltpu.make_async_copy(s, d, load_sem.at[i]) for i, (s, d) in enumerate(loads)]
    for copy in loads:
        copy.start()

    barrier = pltpu.get_barrier_semaphore()

    def greet_dof(k, carry):
        peer = lax.rem(me_p + k, ndof)
        pl.semaphore_signal(barrier, inc=1, device_id=(peer, me_t), device_id_type=MESH)
        return carry

    def greet_dir(k, carry):
        peer = lax.rem(me_t + k, ndir)
        pl.semaphore_signal(barrier, inc=1, device_id=(me_p, peer), device_id_type=MESH)
        return carry

    lax.fori_loop(1, ndof, greet_dof, 0)
    lax.fori_loop(1, ndir, greet_dir, 0)

    lane = iota((SUB, LANES), 1)
    sub = iota((SUB, LANES), 0)

    def at_tile(t):
        return pl.ds(pl.multiple_of(t * LANES, LANES), LANES)

    columns = []
    for q in range(2):
        column = jnp.zeros((SUB, LANES), jnp.float32)
        for kind, table in enumerate((damper_k, damper_c)):
            for i in range(2):
                for j in range(2):
                    column = jnp.where(sub == 4 * kind + 2 * i + j, table[i, j, q], column)
        columns.append(column)
    for copy in loads[2:]:
        copy.wait()
    for t in range(tiles):
        where = slice(t * LANES, (t + 1) * LANES)
        dense = jnp.zeros((SUB, LANES), jnp.float32)
        for q in range(2):
            place = damper_at[q] - me_p * nodes - t * LANES
            dense = dense + jnp.where(lane == place, columns[q], 0.0)
        coef[12, :, where] = dense
        row = offset_raw[t : t + 1, :].astype(jnp.float32)
        coef[13, :, where] = jnp.broadcast_to(row, (SUB, LANES))
    for half in range(2):
        coef[8 + half, 0:4, 0:nodes] = link_raw[2 * half]
        coef[8 + half, 4:8, 0:nodes] = link_raw[2 * half + 1]
        coef[10 + half, 0:4, 0:nodes] = inv_raw[2 * half]
        coef[10 + half, 4:8, 0:nodes] = inv_raw[2 * half + 1]
    for copy in loads[:2]:
        copy.wait()

    groups = dirs // SUB
    packs = []
    for ref in (disp_a, vel):
        for g in range(groups):
            packs.append([(ref, c, slice(g * SUB, (g + 1) * SUB)) for c in range(4)])
    for g in range(0, 14, 4):
        packs.append([(coef, k, slice(0, SUB)) for k in range(g, min(g + 4, 14))])
    for side, start, first in ((0, nodes - LANES, LANES - REACH), (1, 0, 0)):
        for n, pack in enumerate(packs):
            held = None
            for s, (ref, c, rows) in enumerate(pack):
                piece = rolled(ref[c, rows, start : start + LANES], REACH * s - first, 1)
                held = piece if held is None else jnp.where(lane >= REACH * s, piece, held)
            to_send[side, n] = held

    pl.semaphore_wait(barrier, ndof - 1 + ndir - 1)
    halo = []
    for side, by in ((0, 1), (1, ndof - 1)):
        halo.append(
            pltpu.make_async_remote_copy(
                src_ref=to_send.at[side],
                dst_ref=arrived.at[side],
                send_sem=halo_send.at[side],
                recv_sem=halo_recv.at[side],
                device_id=(lax.rem(me_p + by, ndof), me_t),
                device_id_type=MESH,
            )
        )
        halo[-1].start()

    def prepare(t):
        now = at_tile(t)
        before = at_tile(lax.rem(t + around - 1, around))
        p_rows, q_rows = [], []
        for i in range(4):
            shifted = jnp.where(
                lane == 0,
                rolled(coef[4 + i, :, before], 1, 1),
                rolled(coef[4 + i, :, now], 1, 1),
            )
            link = coef[8 + i // 2, :, now]
            if i % 2 == 0:
                link = rolled(link, 4, 0)
            q_rows.append(jnp.where(sub < 4, shifted, link))
            p_rows.append(coef[i, :, now] + jnp.where(sub < 4, rolled(shifted, 4, 0), 0.0))
        film = coef[12, :, now]
        for k in range(2):
            p_rows[k] = p_rows[k] + jnp.where(sub < 2, rolled(film, -2 * k, 0), 0.0)
        v_rows = [rolled(film, -4 - 2 * k, 0) for k in range(2)]
        for i in range(4):
            inv = [
                -coef[10 + i // 2, 4 * (i % 2) + k : 4 * (i % 2) + k + 1, now] for k in range(4)
            ]
            for out, rows in ((pm, p_rows), (qm, q_rows), (vm, v_rows)):
                total = inv[0] * rows[0]
                for k in range(1, len(rows)):
                    total = total + inv[k] * rows[k]
                out[i, :, now] = total

    chunk = min(16, dirs)

    def evaluate(disp, t, finish):
        now = at_tile(t)
        before = at_tile(lax.rem(t + around - 1, around))
        after = at_tile(lax.rem(t + 1, around))
        wide_lane = iota((chunk, LANES), 1)
        target = coef[13, 0:1, now].astype(jnp.int32) + lane[0:1, :]
        inside = jnp.broadcast_to((target >= 0) & (target < LANES), (chunk, LANES))
        index = jnp.broadcast_to(target & (LANES - 1), (chunk, LANES))
        for r in range(0, dirs, chunk):
            rows = slice(r, r + chunk)
            speed = [vel[j, rows, now] for j in range(2)]
            acc = [None] * 4
            for j in range(4):
                here = disp[j, rows, now]
                left = disp[j, rows, before]
                right = disp[j, rows, after]
                previous = jnp.where(wide_lane == 0, rolled(left, 1, 1), rolled(here, 1, 1))
                following = jnp.where(
                    wide_lane == LANES - 1, rolled(right, -1, 1), rolled(here, -1, 1)
                )
                other = jnp.where(wide_lane < LANES // 2, right, left)
                linked = jnp.where(inside, lane_gather(here, index), lane_gather(other, index))
                for i in range(4):
                    total = pm[i, j : j + 1, now] * here
                    total = total + pm[i, 4 + j : 5 + j, now] * following
                    total = total + qm[i, j : j + 1, now] * previous
                    total = total + qm[i, 4 + j : 5 + j, now] * linked
                    if j < 2:
                        total = total + vm[i, j : j + 1, now] * speed[j]
                    acc[i] = total if acc[i] is None else acc[i] + total
            finish(rows, now, acc)

    def finish_first(rows, now, acc):
        for i in range(4):
            v = vel[i, rows, now]
            disp_b[i, rows, now] = (
                disp_a[i, rows, now] + STEP * v + (0.5 * STEP * STEP) * acc[i]
            )
            vel[i, rows, now] = v + (0.5 * STEP) * acc[i]

    def finish_second(rows, now, acc):
        for i in range(4):
            v = vel[i, rows, now] + (0.5 * STEP) * acc[i]
            disp_a[i, rows, now] = (
                disp_b[i, rows, now] + STEP * v + (0.5 * STEP * STEP) * acc[i]
            )
            vel[i, rows, now] = v + (0.5 * STEP) * acc[i]

    def finish_last(rows, now, acc):
        for i in range(4):
            vel[i, rows, now] = vel[i, rows, now] + (0.5 * STEP) * acc[i]

    def prepare_tile(t, carry):
        prepare(t)
        return carry

    def first_tile(t, carry):
        evaluate(disp_a, t, finish_first)
        return carry

    lax.fori_loop(1, tiles, prepare_tile, 0)
    lax.fori_loop(1, tiles - 1, first_tile, 0)

    for copy in halo:
        copy.wait_recv()
    right_end = jnp.where(me_p < ndof - 1, REACH, 0)
    left_start = jnp.where(me_p > 0, LANES - REACH, LANES)
    for n, pack in enumerate(packs):
        from_left, from_right = arrived[0, n], arrived[1, n]
        for s, (ref, c, rows) in enumerate(pack):
            piece = jnp.where(lane < right_end, rolled(from_right, -REACH * s, 1), 0.0)
            ref[c, rows, nodes : nodes + LANES] = jnp.where(
                lane >= left_start, rolled(from_left, LANES - REACH - REACH * s, 1), piece
            )

    def wrapped(k):
        return lax.rem(k, around)

    lax.fori_loop(tiles, tiles + 2, lambda k, c: prepare_tile(wrapped(k), c), 0)
    lax.fori_loop(tiles - 1, tiles + 2, lambda k, c: first_tile(wrapped(k), c), 0)

    def tile_copy(peer):
        return pltpu.make_async_remote_copy(
            src_ref=disp_a.at[:, :, at_tile(peer)],
            dst_ref=x_all.at[:, pl.ds(pl.multiple_of(me_t * dirs, dirs), dirs), :],
            send_sem=a2a_send.at[peer],
            recv_sem=a2a_recv.at[me_t],
            device_id=(me_p, peer),
            device_id_type=MESH,
        )

    def second_tile(by, carry):
        t = lax.rem(me_t + by, ndir)
        evaluate(disp_b, t, finish_second)
        tile_copy(t).start()
        return carry

    half = ndir // 2
    lax.fori_loop(half, ndir, second_tile, 0)
    lax.fori_loop(1, half, lambda k, c: second_tile(half - k, c), 0)
    evaluate(disp_b, me_t, finish_second)
    x_all[:, pl.ds(pl.multiple_of(me_t * dirs, dirs), dirs), :] = disp_a[:, :, at_tile(me_t)]
    evaluate(disp_b, tiles, finish_second)

    def last_tile(t, carry):
        evaluate(disp_a, t, finish_last)
        return carry

    lax.fori_loop(0, tiles, last_tile, 0)
    vel_store = pltpu.make_async_copy(vel.at[:, :, 0:nodes], vel_out, store_sem.at[0])
    vel_store.start()

    def tile_arrival(by):
        source = lax.rem(me_t + by, ndir)
        return pltpu.make_async_remote_copy(
            src_ref=disp_a.at[:, :, at_tile(source)],
            dst_ref=x_all.at[:, pl.ds(pl.multiple_of(source * dirs, dirs), dirs), :],
            send_sem=a2a_send.at[source],
            recv_sem=a2a_recv.at[source],
            device_id=(me_p, source),
            device_id_type=MESH,
        )

    for by in range(1, ndir):
        tile_arrival(by).wait_recv()
    x_store = pltpu.make_async_copy(x_all, x_out, store_sem.at[1])
    x_store.start()

    total = None
    for c in range(4):
        product = lax.dot_general(
            x_all[c],
            x_all[c],
            (((1,), (1,)), ((), ())),
            precision=HIGHEST,
            preferred_element_type=jnp.float32,
        )
        total = product if total is None else total + product
    gram_part[...] = total

    def part_copy(by, source):
        peer = lax.rem(me_t + by, ndir)
        return pltpu.make_async_remote_copy(
            src_ref=gram_part.at[pl.ds(pl.multiple_of(peer * dirs, dirs), dirs), :],
            dst_ref=dir_slots.at[source],
            send_sem=rs_send.at[by],
            recv_sem=rs_recv.at[source],
            device_id=(me_p, peer),
            device_id_type=MESH,
        )

    for by in range(1, ndir):
        part_copy(by, me_t).start()
    dir_slots[me_t] = gram_part[pl.ds(pl.multiple_of(me_t * dirs, dirs), dirs), :]
    for by in range(1, ndir):
        part_copy(by, lax.rem(me_t + by, ndir)).wait_recv()
    total = dir_slots[0]
    for k in range(1, ndir):
        total = total + dir_slots[k]
    dir_sum[...] = total

    def row_copy(by, source):
        peer = lax.rem(me_p + by, ndof)
        return pltpu.make_async_remote_copy(
            src_ref=dir_sum.at[pl.ds(peer * per_dof, per_dof), :],
            dst_ref=dof_slots.at[pl.ds(source * per_dof, per_dof), :],
            send_sem=ds_send.at[by],
            recv_sem=ds_recv.at[source],
            device_id=(peer, me_t),
            device_id_type=MESH,
        )

    def start_row(by, carry):
        row_copy(by, me_p).start()
        return carry

    def await_row(by, carry):
        row_copy(by, lax.rem(me_p + by, ndof)).wait_recv()
        return carry

    lax.fori_loop(1, ndof, start_row, 0)
    dof_slots[pl.ds(me_p * per_dof, per_dof), :] = dir_sum[pl.ds(me_p * per_dof, per_dof), :]
    lax.fori_loop(1, ndof, await_row, 0)
    if per_dof == 1:
        total = jnp.sum(dof_slots[...], axis=0, keepdims=True)
    else:
        total = dof_slots[0:per_dof, :]
        for k in range(1, ndof):
            total = total + dof_slots[k * per_dof : (k + 1) * per_dof, :]
    gram[pl.ds(me_t * dirs + me_p * per_dof, per_dof), :] = total

    def sum_copy(by, source):
        peer = lax.rem(me_p + by, ndof)
        own = pl.ds(me_t * dirs + source * per_dof, per_dof)
        return pltpu.make_async_remote_copy(
            src_ref=gram.at[own, :],
            dst_ref=gram.at[own, :],
            send_sem=dg_send.at[by],
            recv_sem=dg_recv.at[source],
            device_id=(peer, me_t),
            device_id_type=MESH,
        )

    def start_sum(by, carry):
        sum_copy(by, me_p).start()
        return carry

    def await_sum(by, carry):
        sum_copy(by, lax.rem(me_p + by, ndof)).wait_recv()
        return carry

    lax.fori_loop(1, ndof, start_sum, 0)
    lax.fori_loop(1, ndof, await_sum, 0)

    def block_copy(by, source):
        peer = lax.rem(me_t + by, ndir)
        own = pl.ds(pl.multiple_of(source * dirs, dirs), dirs)
        return pltpu.make_async_remote_copy(
            src_ref=gram.at[own, :],
            dst_ref=gram.at[own, :],
            send_sem=ag_send.at[by],
            recv_sem=ag_recv.at[source],
            device_id=(me_p, peer),
            device_id_type=MESH,
        )

    for by in range(1, ndir):
        block_copy(by, me_t).start()
    for by in range(1, ndir):
        block_copy(by, lax.rem(me_t + by, ndir)).wait_recv()
    gram_store = pltpu.make_async_copy(gram, gram_out, store_sem.at[2])
    gram_store.start()

    for copy in halo:
        copy.wait_send()
    for by in range(1, ndir):
        tile_copy(lax.rem(me_t + by, ndir)).wait_send()
        part_copy(by, me_t).wait_send()
        block_copy(by, me_t).wait_send()

    def sent_rows(by, carry):
        row_copy(by, me_p).wait_send()
        sum_copy(by, me_p).wait_send()
        return carry

    lax.fori_loop(1, ndof, sent_rows, 0)
    vel_store.wait()
    x_store.wait()
    gram_store.wait()


def newmark(ndof, ndir, *args):
    dirs, nodes = args[0].shape[1:]
    around = nodes + LANES
    n = dirs * ndir
    packs = 2 * (dirs // SUB) + 4
    f32 = jnp.float32
    hbm = pl.BlockSpec(memory_space=pl.ANY)
    smem = pl.BlockSpec(memory_space=pltpu.SMEM)
    dma = pltpu.SemaphoreType.DMA
    return pl.pallas_call(
        functools.partial(newmark_kernel, ndof, ndir),
        out_shape=(
            jax.ShapeDtypeStruct((4, dirs, nodes), f32),
            jax.ShapeDtypeStruct((4, n, LANES), f32),
            jax.ShapeDtypeStruct((n, n), f32),
        ),
        in_specs=[hbm] * 6 + [smem] * 3,
        out_specs=[hbm] * 3,
        scratch_shapes=[
            pltpu.VMEM((4, dirs, around), f32),
            pltpu.VMEM((4, dirs, around), f32),
            pltpu.VMEM((4, dirs, around), f32),
            pltpu.VMEM((14, SUB, around), f32),
            pltpu.VMEM((4, 4, nodes), f32),
            pltpu.VMEM((4, 4, nodes), f32),
            pltpu.VMEM((nodes // LANES, LANES), jnp.int32),
            pltpu.VMEM((4, SUB, around), f32),
            pltpu.VMEM((4, SUB, around), f32),
            pltpu.VMEM((4, SUB, around), f32),
            pltpu.VMEM((2, packs, SUB, LANES), f32),
            pltpu.VMEM((2, packs, SUB, LANES), f32),
            pltpu.VMEM((4, n, LANES), f32),
            pltpu.VMEM((n, n), f32),
            pltpu.VMEM((ndir, dirs, n), f32),
            pltpu.VMEM((dirs, n), f32),
            pltpu.VMEM((dirs, n), f32),
            pltpu.VMEM((n, n), f32),
            dma((6,)),
            dma((2,)),
            dma((2,)),
            dma((ndir,)),
            dma((ndir,)),
            dma((ndir,)),
            dma((ndir,)),
            dma((ndof,)),
            dma((ndof,)),
            dma((ndof,)),
            dma((ndof,)),
            dma((ndir,)),
            dma((ndir,)),
            dma((3,)),
        ],
        compiler_params=pltpu.CompilerParams(
            collective_id=0, has_side_effects=True, vmem_limit_bytes=48 * 2**20
        ),
        name="newmark_and_gram",
    )(*args)


def spread(x, lane):
    return jnp.broadcast_to(x[:, lane : lane + 1], (x.shape[0], LANES))


def tiled(x, width):
    return x if width == LANES else jnp.concatenate([x] * (width // LANES), axis=1)


def eliminate(block, micro):
    size, width = block.shape
    row = iota((micro, LANES), 0)
    done = []
    for s in range(0, size, micro):
        top = block[0:micro]
        rest = [block[i : i + SUB] for i in range(micro, size - s, SUB)]
        column = [spread(top, s + j) for j in range(micro)]
        inverse = []
        pivots = jnp.broadcast_to(column[0][0:1], (micro, LANES))
        for j in range(micro):
            pivot = column[j][j : j + 1]
            inverse.append(1.0 / pivot)
            pivots = jnp.where(row == j, pivot, pivots)
            if j == micro - 1:
                break
            factor = jnp.where(row > j, column[j] * inverse[j], 0.0)
            for m in range(j + 1, micro):
                column[m] = column[m] - factor * column[m][j : j + 1]
            top = top - tiled(factor, width) * top[j : j + 1]
        below = []
        for part in rest:
            own = [spread(part, s + j) for j in range(micro)]
            for j in range(micro):
                factor = own[j] * inverse[j]
                for m in range(j + 1, micro):
                    own[m] = own[m] - factor * column[m][j : j + 1]
                part = part - tiled(factor, width) * top[j : j + 1]
            below.append(part)
        done.append(top * tiled(lax.rsqrt(pivots), width))
        if below:
            block = jnp.concatenate(below, axis=0) if len(below) > 1 else below[0]
    return jnp.concatenate(done, axis=0)


def factor_kernel(scale, size, micro, gram, x, q_out, r_out, work):
    n = gram.shape[0]
    row, col = iota((size, size), 0), iota((size, size), 1)
    identity = (row == col).astype(jnp.float32)
    work[:, 0:n] = gram[...] * scale
    for c in range(4):
        work[:, n + LANES * c : n + LANES * (c + 1)] = x[c]
    for low in range(0, n, size):
        high = low + size
        block = jnp.concatenate([work[low:high, low:high], identity], axis=1)
        block = eliminate(block, micro)
        later = jnp.dot(
            block[:, size:],
            work[low:high, high:],
            precision=HIGHEST,
            preferred_element_type=jnp.float32,
        )
        if low > 0:
            r_out[low:high, 0:low] = jnp.zeros((size, low), jnp.float32)
        r_out[low:high, low:high] = jnp.where(row <= col, block[:, 0:size], 0.0)
        if high < n:
            r_out[low:high, high:n] = later[:, 0 : n - high]
            work[high:, high:] = work[high:, high:] - lax.dot_general(
                later[:, 0 : n - high],
                later,
                (((0,), (0,)), ((), ())),
                precision=HIGHEST,
                preferred_element_type=jnp.float32,
            )
        for c in range(4):
            start = n - high + LANES * c
            q_out[c, low:high, :] = later[:, start : start + LANES]


def factor(gram, x, scale):
    n = gram.shape[0]
    vmem = pl.BlockSpec(memory_space=pltpu.VMEM)
    return pl.pallas_call(
        functools.partial(factor_kernel, scale, n // 2, SUB),
        out_shape=(
            jax.ShapeDtypeStruct(x.shape, jnp.float32),
            jax.ShapeDtypeStruct((n, n), jnp.float32),
        ),
        in_specs=[vmem, vmem],
        out_specs=[vmem, vmem],
        scratch_shapes=[pltpu.VMEM((n, n + 4 * LANES), jnp.float32)],
        compiler_params=pltpu.CompilerParams(vmem_limit_bytes=32 * 2**20),
        name="factor_and_solve",
    )(gram, x)


def on_device(ndof, ndir, disp, veloc, elem, link, inv, offset, damper_at, damper_k, damper_c):
    nodes = disp.shape[2]
    offset = offset.reshape(nodes // LANES, LANES)
    veloc, x, gram = newmark(
        ndof, ndir, disp, veloc, elem, link, inv, offset, damper_at, damper_k, damper_c
    )
    q_block, r_factor = factor(gram, x, 1.0 / (4.0 * nodes * ndof))
    return veloc, q_block, r_factor


def solution(mesh):
    in_specs = (
        P(None, "dir", "dof"),
        P(None, "dir", "dof"),
        P(None, None, "dof"),
        P(None, None, "dof"),
        P(None, None, "dof"),
        P("dof"),
        P("dof"),
        P(None, None, "dof"),
        P(None, None, "dof"),
    )
    out_specs = (P(None, "dir", "dof"), P(None, None, ("dof", "dir")), P())
    return jax.shard_map(
        functools.partial(on_device, mesh.shape["dof"], mesh.shape["dir"]),
        mesh=mesh,
        in_specs=in_specs,
        out_specs=out_specs,
        check_vma=False,
    )
```

time: 630 us -> 68.1 us (0.11); the launches traced: 623 us -> 67.7 us
  waiting for transfers between devices: 254 us -> 0 us
  local copies, waits for them, and re-layouts: 163 us -> 8.2 us
  other arithmetic: 147 us -> 0 us
  Pallas kernels: 0 us -> 58.8 us
  starting transfers between devices: 36.7 us -> 0 us
  between operations: 16.7 us -> 0.66 us
    psum x1 -> x0, waiting for transfers between devices: 254 us -> none  [on_device(): gram_matrix = lax.psum(gram_local, ('dof', 'dir'))]
    pallas_call x0 -> x2, Pallas kernels: none -> 58.8 us  [the longest x1 49 us: newmark(): pl.pallas_call(functools.partial(newmark_kernel, ndof, ndir), out_shape=(...]
    another operation x15 -> x0, other arithmetic: 56.7 us -> none  [the longest x7 34.6 us: on_device(): lower_factor = jnp.linalg.cholesky(gram_matrix / rows_total)]
    slice x36 -> x0, local copies, waits for them, and re-layouts: 35.3 us -> none  [the longest x19 20.3 us: apply_block(): summed = block[:, 0, None, :] * field[0][None]]
    add x12 -> x0, other arithmetic: 34 us -> none  [the longest x2 13.4 us: on_device(): disp = disp + time_step * veloc + 0.5 * time_step * time_step * accel]
    mul x31 -> x0, local copies, waits for them, and re-layouts: 30.7 us -> none  [the longest x21 19.3 us: apply_block(): summed = summed + block[:, column, None, :] * field[column][None]]
    ppermute x9 -> x0, starting transfers between devices: 30.1 us -> none  [the longest x3 15.1 us: padded_2(): before = lax.ppermute(last, axis, up)]
    gather x9 -> x0, local copies, waits for them, and re-layouts: 29.7 us -> none  [the longest x3 20.9 us: forces(): linked = jnp.take(padded, partner, axis=2)]
  transfers between devices with their start and end apart: 11 -> 0, of which waited for: 1 -> 0; matrix products, arithmetic and copies ran while one was open for 21% -> 0% of each run, Pallas kernels for 0% -> 0%
where the time goes in v1:
time: 68.1 us; the launch traced here: 67.7 us
  Pallas kernels  58.8 us (86%)
  local copies, waits for them, and re-layouts  8.2 us (12%)
    pallas_call x1, Pallas kernels, newmark(): pl.pallas_call(functools.partial(newmark_kernel, ndof, ndir), out_shape=(...  49 us
    pallas_call x1, Pallas kernels, factor(): pl.pallas_call(functools.partial(factor_kernel, scale, n // 2, SUB), out_...  9.85 us
    unnamed x19, local copies, waits for them, and re-layouts  8.2 us

profile of v1, /device:TPU:1, one launch (start us, length us, event | category | flops | bytes accessed | tf_op | source)
XLA Modules:
  0.0 67.7 jit_solution(2473855320630573773)
XLA Ops:
  0.6 0.0 copy-start.8
  0.6 0.6 copy-done.8
  1.3 0.0 copy-start
  1.3 1.0 %copy-done = f32[4,32,1024]{2,1,0:T(8,128)S(1)} copy-done((f32[4,32,1024]{2,1,0:T(8,128)S(1)}, f32[4,32,1024]{2,1,0:T(8,128)}, u32[]{:S(2)}) %copy-start) | copy-done | bytes 524312
  2.3 0.0 copy-start.1
  2.3 1.0 %copy-done.1 = f32[4,32,1024]{2,1,0:T(8,128)S(1)} copy-done((f32[4,32,1024]{2,1,0:T(8,128)S(1)}, f32[4,32,1024]{2,1,0:T(8,128)}, u32[]{:S(2)}) %copy-start.1) | copy-done | bytes 524312
  3.4 0.0 copy-start.2
  3.4 0.9 %copy-done.2 = f32[8,8,1024]{2,1,0:T(8,128)S(1)} copy-done((f32[8,8,1024]{2,1,0:T(8,128)S(1)}, f32[8,8,1024]{2,1,0:T(8,128)}, u32[]{:S(2)}) %copy-start.2) | copy-done | bytes 262168
  4.3 0.0 copy-start.3
  4.3 0.8 %copy-done.3 = f32[4,4,1024]{2,1,0:T(4,128)S(1)} copy-done((f32[4,4,1024]{2,1,0:T(4,128)S(1)}, f32[4,4,1024]{2,1,0:T(4,128)}, u32[]{:S(2)}) %copy-start.3) | copy-done | bytes 65560
  5.2 0.0 copy-start.4
  5.2 0.8 %copy-done.4 = f32[4,4,1024]{2,1,0:T(4,128)S(1)} copy-done((f32[4,4,1024]{2,1,0:T(4,128)S(1)}, f32[4,4,1024]{2,1,0:T(4,128)}, u32[]{:S(2)}) %copy-start.4) | copy-done | bytes 65560
  6.0 0.0 copy-start.5
  6.0 0.7 %copy-done.5 = s32[1024]{0:T(1024)S(1)} copy-done((s32[1024]{0:T(1024)S(1)}, s32[1024]{0:T(1024)}, u32[]{:S(2)}) %copy-start.5) | copy-done | bytes 4120
  6.7 0.0 copy-start.6
  6.7 0.7 %copy-done.6 = f32[2,2,2]{2,1,0:T(2,128)S(1)} copy-done((f32[2,2,2]{2,1,0:T(2,128)S(1)}, f32[2,2,2]{2,1,0:T(2,128)}, u32[]{:S(2)}) %copy-start.6) | copy-done | bytes 56
  7.4 0.0 copy-start.7
  7.4 0.7 %copy-done.7 = f32[2,2,2]{2,1,0:T(2,128)S(1)} copy-done((f32[2,2,2]{2,1,0:T(2,128)S(1)}, f32[2,2,2]{2,1,0:T(2,128)}, u32[]{:S(2)}) %copy-start.7) | copy-done | bytes 56
  8.1 49.0 %newmark_and_gram.1 = (f32[4,32,1024]{2,1,0:T(8,128)S(1)}, f32[4,256,128]{2,1,0:T(8,128)S(1)}, f32[256,256]{1,0:T(8,128)S(1)}) custom-call(f32[4,32,1024]{2,1,0:T(8,128)S(1)} %copy-done, f32[4,32,1024]{2,1,0:T(8,128)S(1)} %copy-done.1, f32[8,8,1024]{2,1,0:T(8,128)S(1)} %copy-done.2, f32[4,4,1024]{2,1,0:T(4,128)S(1)} %copy-done.3, ...), custom_call_target="tpu_custom_call" | custom-call | tf_op jit(solution)/shard_map/newmark_and_gram/pallas_call | solution.py:468
  57.0 9.9 %factor_and_solve.1 = (f32[4,256,128]{2,1,0:T(8,128)}, f32[256,256]{1,0:T(8,128)}) custom-call(f32[256,256]{1,0:T(8,128)S(1)} %get-tuple-element.9.gram, f32[4,256,128]{2,1,0:T(8,128)S(1)} %get-tuple-element.10.x), custom_call_target="tpu_custom_call" | custom-call | tf_op jit(solution)/shard_map/factor_and_solve/pallas_call | solution.py:598
  66.9 0.8 %copy.13 = f32[4,32,1024]{2,1,0:T(8,128)} copy(f32[4,32,1024]{2,1,0:T(8,128)S(1)} %get-tuple-element.16) | data formatting | bytes 1048576
Async XLA Ops:
  0.6 0.7 copy-start.8
  1.3 1.0 %copy-start = (f32[4,32,1024]{2,1,0:T(8,128)S(1)}, f32[4,32,1024]{2,1,0:T(8,128)}, u32[]{:S(2)}) copy-start(f32[4,32,1024]{2,1,0:T(8,128)} %disp_in.1) | copy-start | bytes 1572868
  2.3 1.0 %copy-start.1 = (f32[4,32,1024]{2,1,0:T(8,128)S(1)}, f32[4,32,1024]{2,1,0:T(8,128)}, u32[]{:S(2)}) copy-start(f32[4,32,1024]{2,1,0:T(8,128)} %vel_in.1) | copy-start | bytes 1572868
  3.4 0.9 %copy-start.2 = (f32[8,8,1024]{2,1,0:T(8,128)S(1)}, f32[8,8,1024]{2,1,0:T(8,128)}, u32[]{:S(2)}) copy-start(f32[8,8,1024]{2,1,0:T(8,128)} %elem_in.1) | copy-start | bytes 786436
  4.3 0.8 %copy-start.3 = (f32[4,4,1024]{2,1,0:T(4,128)S(1)}, f32[4,4,1024]{2,1,0:T(4,128)}, u32[]{:S(2)}) copy-start(f32[4,4,1024]{2,1,0:T(4,128)} %link_in.1) | copy-start | bytes 196612
  5.2 0.8 %copy-start.4 = (f32[4,4,1024]{2,1,0:T(4,128)S(1)}, f32[4,4,1024]{2,1,0:T(4,128)}, u32[]{:S(2)}) copy-start(f32[4,4,1024]{2,1,0:T(4,128)} %inv_in.1) | copy-start | bytes 196612
  6.0 0.7 %copy-start.5 = (s32[1024]{0:T(1024)S(1)}, s32[1024]{0:T(1024)}, u32[]{:S(2)}) copy-start(s32[1024]{0:T(1024)} %param.14) | copy-start | bytes 12292
  6.7 0.7 %copy-start.6 = (f32[2,2,2]{2,1,0:T(2,128)S(1)}, f32[2,2,2]{2,1,0:T(2,128)}, u32[]{:S(2)}) copy-start(f32[2,2,2]{2,1,0:T(2,128)} %damper_k.1) | copy-start | bytes 100
  7.4 0.7 %copy-start.7 = (f32[2,2,2]{2,1,0:T(2,128)S(1)}, f32[2,2,2]{2,1,0:T(2,128)}, u32[]{:S(2)}) copy-start(f32[2,2,2]{2,1,0:T(2,128)} %damper_c.1) | copy-start | bytes 100

commit v2 on v1

--- a/solution.py
+++ b/solution.py
@@ -11,6 +11,7 @@
 LANES = 128
 SUB = 8
 REACH = 32
+CHIPS_X = 4
 MESH = pl.DeviceIdType.MESH
 HIGHEST = lax.Precision.HIGHEST
 
@@ -28,8 +29,16 @@
     return jnp.take_along_axis(x, index, axis=1, mode="promise_in_bounds")
 
 
+def far_first(offsets, sizes):
+    def distance(offset):
+        return sum(min(o, n - o) for o, n in zip(offset, sizes))
+
+    return [o for o in sorted(offsets, key=distance, reverse=True) if distance(o)]
+
+
 def newmark_kernel(
     ndof,
+    nx,
     ndir,
     disp_in,
     vel_in,
@@ -57,9 +66,10 @@
     arrived,
     x_all,
     gram_part,
-    dir_slots,
-    dir_sum,
-    dof_slots,
+    slots,
+    z_part,
+    z_slots,
+    z_sum,
     gram,
     load_sem,
     halo_send,
@@ -68,10 +78,8 @@
     a2a_recv,
     rs_send,
     rs_recv,
-    ds_send,
-    ds_recv,
-    dg_send,
-    dg_recv,
+    z_send,
+    z_recv,
     ag_send,
     ag_recv,
     store_sem,
@@ -82,7 +90,12 @@
     nodes = disp_in.shape[2]
     tiles = nodes // LANES
     around = tiles + 1
-    per_dof = dirs // ndof
+    nz = ndof // nx
+    me_z, me_x = me_p // nx, lax.rem(me_p, nx)
+    me = me_t * nx + me_x
+    share = gram.shape[1] // (nx * ndir)
+    plane = far_first([(x, t) for x in range(nx) for t in range(ndir)], (nx, ndir))
+    line = [by for by, in far_first([(z,) for z in range(nz)], (nz,))]
 
     loads = [
         (disp_in, disp_a.at[:, :, 0:nodes]),
@@ -98,18 +111,15 @@
 
     barrier = pltpu.get_barrier_semaphore()
 
-    def greet_dof(k, carry):
-        peer = lax.rem(me_p + k, ndof)
-        pl.semaphore_signal(barrier, inc=1, device_id=(peer, me_t), device_id_type=MESH)
-        return carry
-
-    def greet_dir(k, carry):
-        peer = lax.rem(me_t + k, ndir)
-        pl.semaphore_signal(barrier, inc=1, device_id=(me_p, peer), device_id_type=MESH)
-        return carry
-
-    lax.fori_loop(1, ndof, greet_dof, 0)
-    lax.fori_loop(1, ndir, greet_dir, 0)
+    def greet(p, t):
+        pl.semaphore_signal(barrier, inc=1, device_id=(p, t), device_id_type=MESH)
+
+    for by in line:
+        greet(lax.rem(me_z + by, nz) * nx + me_x, me_t)
+    for by in (1, ndof - 1):
+        greet(lax.rem(me_p + by, ndof), me_t)
+    for by_x, by_t in plane:
+        greet(me_z * nx + lax.rem(me_x + by_x, nx), lax.rem(me_t + by_t, ndir))
 
     lane = iota((SUB, LANES), 1)
     sub = iota((SUB, LANES), 0)
@@ -159,7 +169,7 @@
                 held = piece if held is None else jnp.where(lane >= REACH * s, piece, held)
             to_send[side, n] = held
 
-    pl.semaphore_wait(barrier, ndof - 1 + ndir - 1)
+    pl.semaphore_wait(barrier, len(line) + 2 + len(plane))
     halo = []
     for side, by in ((0, 1), (1, ndof - 1)):
         halo.append(
@@ -333,108 +343,89 @@
     x_store = pltpu.make_async_copy(x_all, x_out, store_sem.at[1])
     x_store.start()
 
-    total = None
-    for c in range(4):
-        product = lax.dot_general(
-            x_all[c],
-            x_all[c],
-            (((1,), (1,)), ((), ())),
-            precision=HIGHEST,
-            preferred_element_type=jnp.float32,
-        )
-        total = product if total is None else total + product
-    gram_part[...] = total
-
-    def part_copy(by, source):
-        peer = lax.rem(me_t + by, ndir)
+    half_n = gram.shape[1]
+    halves = [slice(0, half_n), slice(half_n, 2 * half_n)]
+    for b, (i, j) in enumerate(((0, 0), (0, 1), (1, 1))):
+        total = None
+        for c in range(4):
+            product = lax.dot_general(
+                x_all[c, halves[i], :],
+                x_all[c, halves[j], :],
+                (((1,), (1,)), ((), ())),
+                precision=HIGHEST,
+                preferred_element_type=jnp.float32,
+            )
+            total = product if total is None else total + product
+        gram_part[b] = total
+
+    def part_copy(by):
+        peer_x, peer_t = by
+        to = lax.rem(me_x + peer_x, nx), lax.rem(me_t + peer_t, ndir)
+        member = to[1] * nx + to[0]
         return pltpu.make_async_remote_copy(
-            src_ref=gram_part.at[pl.ds(pl.multiple_of(peer * dirs, dirs), dirs), :],
-            dst_ref=dir_slots.at[source],
-            send_sem=rs_send.at[by],
-            recv_sem=rs_recv.at[source],
-            device_id=(me_p, peer),
+            src_ref=gram_part.at[:, pl.ds(member * share, share), :],
+            dst_ref=slots.at[:, pl.ds(me * share, share), :],
+            send_sem=rs_send,
+            recv_sem=rs_recv,
+            device_id=(me_z * nx + to[0], to[1]),
             device_id_type=MESH,
         )
 
-    for by in range(1, ndir):
-        part_copy(by, me_t).start()
-    dir_slots[me_t] = gram_part[pl.ds(pl.multiple_of(me_t * dirs, dirs), dirs), :]
-    for by in range(1, ndir):
-        part_copy(by, lax.rem(me_t + by, ndir)).wait_recv()
-    total = dir_slots[0]
-    for k in range(1, ndir):
-        total = total + dir_slots[k]
-    dir_sum[...] = total
-
-    def row_copy(by, source):
-        peer = lax.rem(me_p + by, ndof)
+    for by in plane:
+        part_copy(by).start()
+    mine = pl.ds(me * share, share)
+    own = pltpu.make_async_copy(gram_part.at[:, mine, :], slots.at[:, mine, :], rs_recv)
+    own.start()
+    pltpu.make_async_copy(slots, slots, rs_recv).wait()
+    total = slots[:, 0:SUB, :]
+    for k in range(SUB, slots.shape[1], SUB):
+        total = total + slots[:, k : k + SUB, :]
+    for b in range(3):
+        piece = total[b]
+        for k in range(share, SUB, share):
+            piece = piece + rolled(total[b], -k, 0)
+        z_part[b] = piece
+
+    def z_copy(by):
         return pltpu.make_async_remote_copy(
-            src_ref=dir_sum.at[pl.ds(peer * per_dof, per_dof), :],
-            dst_ref=dof_slots.at[pl.ds(source * per_dof, per_dof), :],
-            send_sem=ds_send.at[by],
-            recv_sem=ds_recv.at[source],
-            device_id=(peer, me_t),
+            src_ref=z_part.at[:, 0:share, :],
+            dst_ref=z_slots.at[me_z, :, 0:share, :],
+            send_sem=z_send,
+            recv_sem=z_recv,
+            device_id=(lax.rem(me_z + by, nz) * nx + me_x, me_t),
             device_id_type=MESH,
         )
 
-    def start_row(by, carry):
-        row_copy(by, me_p).start()
-        return carry
-
-    def await_row(by, carry):
-        row_copy(by, lax.rem(me_p + by, ndof)).wait_recv()
-        return carry
-
-    lax.fori_loop(1, ndof, start_row, 0)
-    dof_slots[pl.ds(me_p * per_dof, per_dof), :] = dir_sum[pl.ds(me_p * per_dof, per_dof), :]
-    lax.fori_loop(1, ndof, await_row, 0)
-    if per_dof == 1:
-        total = jnp.sum(dof_slots[...], axis=0, keepdims=True)
-    else:
-        total = dof_slots[0:per_dof, :]
-        for k in range(1, ndof):
-            total = total + dof_slots[k * per_dof : (k + 1) * per_dof, :]
-    gram[pl.ds(me_t * dirs + me_p * per_dof, per_dof), :] = total
-
-    def sum_copy(by, source):
-        peer = lax.rem(me_p + by, ndof)
-        own = pl.ds(me_t * dirs + source * per_dof, per_dof)
+    for by in line:
+        z_copy(by).start()
+    own = pltpu.make_async_copy(
+        z_part.at[:, 0:share, :], z_slots.at[me_z, :, 0:share, :], z_recv
+    )
+    own.start()
+    arrivals = z_slots.at[:, :, 0:share, :]
+    pltpu.make_async_copy(arrivals, arrivals, z_recv).wait()
+    total = z_slots[0, :, 0:share, :]
+    for k in range(1, nz):
+        total = total + z_slots[k, :, 0:share, :]
+    z_sum[:, 0:share, :] = total
+
+    def sum_copy(by):
+        peer_x, peer_t = by
+        to = lax.rem(me_x + peer_x, nx), lax.rem(me_t + peer_t, ndir)
         return pltpu.make_async_remote_copy(
-            src_ref=gram.at[own, :],
-            dst_ref=gram.at[own, :],
-            send_sem=dg_send.at[by],
-            recv_sem=dg_recv.at[source],
-            device_id=(peer, me_t),
+            src_ref=z_sum.at[:, 0:share, :],
+            dst_ref=gram.at[:, mine, :],
+            send_sem=ag_send,
+            recv_sem=ag_recv,
+            device_id=(me_z * nx + to[0], to[1]),
             device_id_type=MESH,
         )
 
-    def start_sum(by, carry):
-        sum_copy(by, me_p).start()
-        return carry
-
-    def await_sum(by, carry):
-        sum_copy(by, lax.rem(me_p + by, ndof)).wait_recv()
-        return carry
-
-    lax.fori_loop(1, ndof, start_sum, 0)
-    lax.fori_loop(1, ndof, await_sum, 0)
-
-    def block_copy(by, source):
-        peer = lax.rem(me_t + by, ndir)
-        own = pl.ds(pl.multiple_of(source * dirs, dirs), dirs)
-        return pltpu.make_async_remote_copy(
-            src_ref=gram.at[own, :],
-            dst_ref=gram.at[own, :],
-            send_sem=ag_send.at[by],
-            recv_sem=ag_recv.at[source],
-            device_id=(me_p, peer),
-            device_id_type=MESH,
-        )
-
-    for by in range(1, ndir):
-        block_copy(by, me_t).start()
-    for by in range(1, ndir):
-        block_copy(by, lax.rem(me_t + by, ndir)).wait_recv()
+    for by in plane:
+        sum_copy(by).start()
+    own = pltpu.make_async_copy(z_sum.at[:, 0:share, :], gram.at[:, mine, :], ag_recv)
+    own.start()
+    pltpu.make_async_copy(gram, gram, ag_recv).wait()
     gram_store = pltpu.make_async_copy(gram, gram_out, store_sem.at[2])
     gram_store.start()
 
@@ -442,35 +433,31 @@
         copy.wait_send()
     for by in range(1, ndir):
         tile_copy(lax.rem(me_t + by, ndir)).wait_send()
-        part_copy(by, me_t).wait_send()
-        block_copy(by, me_t).wait_send()
-
-    def sent_rows(by, carry):
-        row_copy(by, me_p).wait_send()
-        sum_copy(by, me_p).wait_send()
-        return carry
-
-    lax.fori_loop(1, ndof, sent_rows, 0)
+    for by in plane:
+        part_copy(by).wait_send()
+        sum_copy(by).wait_send()
+    for by in line:
+        z_copy(by).wait_send()
     vel_store.wait()
     x_store.wait()
     gram_store.wait()
 
 
-def newmark(ndof, ndir, *args):
+def newmark(ndof, nx, ndir, *args):
     dirs, nodes = args[0].shape[1:]
     around = nodes + LANES
     n = dirs * ndir
     packs = 2 * (dirs // SUB) + 4
     f32 = jnp.float32
-    hbm = pl.BlockSpec(memory_space=pl.ANY)
+    hbm = pl.BlockSpec(memory_space=pltpu.HBM)
     smem = pl.BlockSpec(memory_space=pltpu.SMEM)
     dma = pltpu.SemaphoreType.DMA
     return pl.pallas_call(
-        functools.partial(newmark_kernel, ndof, ndir),
+        functools.partial(newmark_kernel, ndof, nx, ndir),
         out_shape=(
             jax.ShapeDtypeStruct((4, dirs, nodes), f32),
             jax.ShapeDtypeStruct((4, n, LANES), f32),
-            jax.ShapeDtypeStruct((n, n), f32),
+            jax.ShapeDtypeStruct((3, n // 2, n // 2), f32),
         ),
         in_specs=[hbm] * 6 + [smem] * 3,
         out_specs=[hbm] * 3,
@@ -488,28 +475,27 @@
             pltpu.VMEM((2, packs, SUB, LANES), f32),
             pltpu.VMEM((2, packs, SUB, LANES), f32),
             pltpu.VMEM((4, n, LANES), f32),
-            pltpu.VMEM((n, n), f32),
-            pltpu.VMEM((ndir, dirs, n), f32),
-            pltpu.VMEM((dirs, n), f32),
-            pltpu.VMEM((dirs, n), f32),
-            pltpu.VMEM((n, n), f32),
+            pltpu.VMEM((3, n // 2, n // 2), f32),
+            pltpu.VMEM((3, n // 2, n // 2), f32),
+            pltpu.VMEM((3, SUB, n // 2), f32),
+            pltpu.VMEM((ndof // nx, 3, SUB, n // 2), f32),
+            pltpu.VMEM((3, SUB, n // 2), f32),
+            pltpu.VMEM((3, n // 2, n // 2), f32),
             dma((6,)),
             dma((2,)),
             dma((2,)),
             dma((ndir,)),
             dma((ndir,)),
-            dma((ndir,)),
-            dma((ndir,)),
-            dma((ndof,)),
-            dma((ndof,)),
-            dma((ndof,)),
-            dma((ndof,)),
-            dma((ndir,)),
-            dma((ndir,)),
+            dma(()),
+            dma(()),
+            dma(()),
+            dma(()),
+            dma(()),
+            dma(()),
             dma((3,)),
         ],
         compiler_params=pltpu.CompilerParams(
-            collective_id=0, has_side_effects=True, vmem_limit_bytes=48 * 2**20
+            collective_id=0, has_side_effects=True, vmem_limit_bytes=62 * 2**20
         ),
         name="newmark_and_gram",
     )(*args)
@@ -558,30 +544,45 @@
     return jnp.concatenate(done, axis=0)
 
 
-def factor_kernel(scale, size, micro, gram, x, q_out, r_out, work):
-    n = gram.shape[0]
+def factor_kernel(scale, micro, gram_in, x_in, vel_in, q_out, r_out, vel_out, gram, work, sems):
+    size = gram.shape[1]
+    n = 2 * size
+    gram_load = pltpu.make_async_copy(gram_in, gram, sems.at[0])
+    gram_load.start()
+    x_loads = [
+        pltpu.make_async_copy(
+            x_in.at[c], work.at[:, n + LANES * c : n + LANES * (c + 1)], sems.at[1 + c]
+        )
+        for c in range(4)
+    ]
+    for copy in x_loads:
+        copy.start()
+    vel_move = pltpu.make_async_copy(vel_in, vel_out, sems.at[5])
+    vel_move.start()
     row, col = iota((size, size), 0), iota((size, size), 1)
     identity = (row == col).astype(jnp.float32)
-    work[:, 0:n] = gram[...] * scale
-    for c in range(4):
-        work[:, n + LANES * c : n + LANES * (c + 1)] = x[c]
+    r_out[size:, 0:size] = jnp.zeros((size, size), jnp.float32)
+    gram_load.wait()
+    work[0:size, size:n] = gram[1] * scale
     for low in range(0, n, size):
         high = low + size
-        block = jnp.concatenate([work[low:high, low:high], identity], axis=1)
-        block = eliminate(block, micro)
+        block = gram[0] * scale if low == 0 else work[low:high, low:high]
+        block = eliminate(jnp.concatenate([block, identity], axis=1), micro)
+        if low == 0:
+            for copy in x_loads:
+                copy.wait()
         later = jnp.dot(
             block[:, size:],
             work[low:high, high:],
             precision=HIGHEST,
             preferred_element_type=jnp.float32,
         )
-        if low > 0:
-            r_out[low:high, 0:low] = jnp.zeros((size, low), jnp.float32)
         r_out[low:high, low:high] = jnp.where(row <= col, block[:, 0:size], 0.0)
-        if high < n:
-            r_out[low:high, high:n] = later[:, 0 : n - high]
+        if low == 0:
+            r_out[low:high, high:n] = later[:, 0:size]
+            work[high:, high:n] = gram[2] * scale
             work[high:, high:] = work[high:, high:] - lax.dot_general(
-                later[:, 0 : n - high],
+                later[:, 0:size],
                 later,
                 (((0,), (0,)), ((), ())),
                 precision=HIGHEST,
@@ -590,32 +591,40 @@
         for c in range(4):
             start = n - high + LANES * c
             q_out[c, low:high, :] = later[:, start : start + LANES]
-
-
-def factor(gram, x, scale):
-    n = gram.shape[0]
+    vel_move.wait()
+
+
+def factor(gram, x, vel, scale):
+    n = x.shape[1]
     vmem = pl.BlockSpec(memory_space=pltpu.VMEM)
+    hbm = pl.BlockSpec(memory_space=pltpu.HBM)
     return pl.pallas_call(
-        functools.partial(factor_kernel, scale, n // 2, SUB),
+        functools.partial(factor_kernel, scale, SUB),
         out_shape=(
             jax.ShapeDtypeStruct(x.shape, jnp.float32),
             jax.ShapeDtypeStruct((n, n), jnp.float32),
+            jax.ShapeDtypeStruct(vel.shape, jnp.float32),
         ),
-        in_specs=[vmem, vmem],
-        out_specs=[vmem, vmem],
-        scratch_shapes=[pltpu.VMEM((n, n + 4 * LANES), jnp.float32)],
-        compiler_params=pltpu.CompilerParams(vmem_limit_bytes=32 * 2**20),
+        in_specs=[hbm, hbm, hbm],
+        out_specs=[vmem, vmem, hbm],
+        scratch_shapes=[
+            pltpu.VMEM(gram.shape, jnp.float32),
+            pltpu.VMEM((n, n + 4 * LANES), jnp.float32),
+            pltpu.SemaphoreType.DMA((6,)),
+        ],
+        compiler_params=pltpu.CompilerParams(vmem_limit_bytes=62 * 2**20),
         name="factor_and_solve",
-    )(gram, x)
+    )(gram, x, vel)
 
 
 def on_device(ndof, ndir, disp, veloc, elem, link, inv, offset, damper_at, damper_k, damper_c):
     nodes = disp.shape[2]
     offset = offset.reshape(nodes // LANES, LANES)
+    nx = CHIPS_X if ndof % CHIPS_X == 0 else 1
     veloc, x, gram = newmark(
-        ndof, ndir, disp, veloc, elem, link, inv, offset, damper_at, damper_k, damper_c
+        ndof, nx, ndir, disp, veloc, elem, link, inv, offset, damper_at, damper_k, damper_c
     )
-    q_block, r_factor = factor(gram, x, 1.0 / (4.0 * nodes * ndof))
+    q_block, r_factor, veloc = factor(gram, x, veloc, 1.0 / (4.0 * nodes * ndof))
     return veloc, q_block, r_factor
 
 

time: 68.1 us -> 59.9 us (0.88)
  local copies, waits for them, and re-layouts: 8.2 us -> 0 us
    unnamed x19 -> x0, local copies, waits for them, and re-layouts: 8.2 us -> none
where the time goes in v2:
time: 59.9 us; the launch traced here: 59.7 us
  Pallas kernels  59.1 us (99%)
  between operations  0.64 us (1%)
    pallas_call x1, Pallas kernels, newmark(): pl.pallas_call(functools.partial(newmark_kernel, ndof, nx, ndir), out_sha...  41.1 us
    pallas_call x1, Pallas kernels, factor(): pl.pallas_call(functools.partial(factor_kernel, scale, SUB), out_shape=(j...  17.9 us

profile of v2, /device:TPU:1, one launch (start us, length us, event | category | flops | bytes accessed | tf_op | source)
XLA Modules:
  0.0 59.7 jit_solution(11562409564230831951)
XLA Ops:
  0.6 41.1 %newmark_and_gram.1 = (f32[4,32,1024]{2,1,0:T(8,128)}, f32[4,256,128]{2,1,0:T(8,128)}, f32[3,128,128]{2,1,0:T(8,128)}) custom-call(f32[4,32,1024]{2,1,0:T(8,128)} %disp_in.1, f32[4,32,1024]{2,1,0:T(8,128)} %vel_in.1, f32[8,8,1024]{2,1,0:T(8,128)} %elem_in.1, f32[4,4,1024]{2,1,0:T(4,128)} %link_in.1, f32[4,4,1024]{2,1,0:T(4,128)} %inv_in.1, ...), custom_call_target="tpu_custom_call" | custom-call | tf_op jit(solution)/shard_map/newmark_and_gram/pallas_call | solution.py:455
  41.8 17.9 %factor_and_solve.1 = (f32[4,256,128]{2,1,0:T(8,128)}, f32[256,256]{1,0:T(8,128)}, f32[4,32,1024]{2,1,0:T(8,128)}) custom-call(f32[3,128,128]{2,1,0:T(8,128)} %get-tuple-element.9.gram_in, f32[4,256,128]{2,1,0:T(8,128)} %get-tuple-element.10.x_in, f32[4,32,1024]{2,1,0:T(8,128)} %get-tuple-element.11.vel_in), custom_call_target="tpu_custom_call" | custom-call | tf_op jit(solution)/shard_map/factor_and_solve/pallas_call | solution.py:601

commit v3 on v2

--- a/solution.py
+++ b/solution.py
@@ -509,13 +509,14 @@
     return x if width == LANES else jnp.concatenate([x] * (width // LANES), axis=1)
 
 
-def eliminate(block, micro):
+def eliminate(block, micro, near):
     size, width = block.shape
     row = iota((micro, LANES), 0)
+    rows = [block[i : i + SUB] for i in range(0, size, SUB)]
     done = []
     for s in range(0, size, micro):
-        top = block[0:micro]
-        rest = [block[i : i + SUB] for i in range(micro, size - s, SUB)]
+        top = jnp.concatenate(rows[: micro // SUB], axis=0)
+        rest = rows[micro // SUB :]
         column = [spread(top, s + j) for j in range(micro)]
         inverse = []
         pivots = jnp.broadcast_to(column[0][0:1], (micro, LANES))
@@ -529,22 +530,34 @@
             for m in range(j + 1, micro):
                 column[m] = column[m] - factor * column[m][j : j + 1]
             top = top - tiled(factor, width) * top[j : j + 1]
-        below = []
-        for part in rest:
+        rows = []
+        for part in rest[:near]:
             own = [spread(part, s + j) for j in range(micro)]
             for j in range(micro):
                 factor = own[j] * inverse[j]
                 for m in range(j + 1, micro):
                     own[m] = own[m] - factor * column[m][j : j + 1]
                 part = part - tiled(factor, width) * top[j : j + 1]
-            below.append(part)
-        done.append(top * tiled(lax.rsqrt(pivots), width))
-        if below:
-            block = jnp.concatenate(below, axis=0) if len(below) > 1 else below[0]
+            rows.append(part)
+        top = top * tiled(lax.rsqrt(pivots), width)
+        if len(rest) > near:
+            update = lax.dot_general(
+                top[:, 0:size],
+                top,
+                (((0,), (0,)), ((), ())),
+                precision=HIGHEST,
+                preferred_element_type=jnp.float32,
+            )
+            for i in range(near, len(rest)):
+                start = s + micro + SUB * i
+                rows.append(rest[i] - update[start : start + SUB])
+        done.append(top)
     return jnp.concatenate(done, axis=0)
 
 
-def factor_kernel(scale, micro, gram_in, x_in, vel_in, q_out, r_out, vel_out, gram, work, sems):
+def factor_kernel(
+    scale, micro, near, gram_in, x_in, vel_in, q_out, r_out, vel_out, gram, vel, q, r, work, sems
+):
     size = gram.shape[1]
     n = 2 * size
     gram_load = pltpu.make_async_copy(gram_in, gram, sems.at[0])
@@ -557,29 +570,33 @@
     ]
     for copy in x_loads:
         copy.start()
-    vel_move = pltpu.make_async_copy(vel_in, vel_out, sems.at[5])
-    vel_move.start()
+    vel_load = pltpu.make_async_copy(vel_in, vel, sems.at[5])
+    vel_load.start()
+    vel_store = pltpu.make_async_copy(vel, vel_out, sems.at[6])
+    stores = []
     row, col = iota((size, size), 0), iota((size, size), 1)
     identity = (row == col).astype(jnp.float32)
-    r_out[size:, 0:size] = jnp.zeros((size, size), jnp.float32)
+    r[size:, 0:size] = jnp.zeros((size, size), jnp.float32)
     gram_load.wait()
     work[0:size, size:n] = gram[1] * scale
     for low in range(0, n, size):
         high = low + size
         block = gram[0] * scale if low == 0 else work[low:high, low:high]
-        block = eliminate(jnp.concatenate([block, identity], axis=1), micro)
+        block = eliminate(jnp.concatenate([block, identity], axis=1), micro, near)
         if low == 0:
             for copy in x_loads:
                 copy.wait()
+            vel_load.wait()
+            vel_store.start()
         later = jnp.dot(
             block[:, size:],
             work[low:high, high:],
             precision=HIGHEST,
             preferred_element_type=jnp.float32,
         )
-        r_out[low:high, low:high] = jnp.where(row <= col, block[:, 0:size], 0.0)
+        r[low:high, low:high] = jnp.where(row <= col, block[:, 0:size], 0.0)
         if low == 0:
-            r_out[low:high, high:n] = later[:, 0:size]
+            r[low:high, high:n] = later[:, 0:size]
             work[high:, high:n] = gram[2] * scale
             work[high:, high:] = work[high:, high:] - lax.dot_general(
                 later[:, 0:size],
@@ -590,27 +607,38 @@
             )
         for c in range(4):
             start = n - high + LANES * c
-            q_out[c, low:high, :] = later[:, start : start + LANES]
-    vel_move.wait()
+            q[c, low:high, :] = later[:, start : start + LANES]
+        part = pl.ds(low, size)
+        stores += [
+            pltpu.make_async_copy(q.at[:, part, :], q_out.at[:, part, :], sems.at[7 + low // size]),
+            pltpu.make_async_copy(r.at[part, :], r_out.at[part, :], sems.at[9 + low // size]),
+        ]
+        for copy in stores[-2:]:
+            copy.start()
+    for copy in stores:
+        copy.wait()
+    vel_store.wait()
 
 
 def factor(gram, x, vel, scale):
     n = x.shape[1]
-    vmem = pl.BlockSpec(memory_space=pltpu.VMEM)
     hbm = pl.BlockSpec(memory_space=pltpu.HBM)
     return pl.pallas_call(
-        functools.partial(factor_kernel, scale, SUB),
+        functools.partial(factor_kernel, scale, 2 * SUB, 2),
         out_shape=(
             jax.ShapeDtypeStruct(x.shape, jnp.float32),
             jax.ShapeDtypeStruct((n, n), jnp.float32),
             jax.ShapeDtypeStruct(vel.shape, jnp.float32),
         ),
         in_specs=[hbm, hbm, hbm],
-        out_specs=[vmem, vmem, hbm],
+        out_specs=[hbm, hbm, hbm],
         scratch_shapes=[
             pltpu.VMEM(gram.shape, jnp.float32),
+            pltpu.VMEM(vel.shape, jnp.float32),
+            pltpu.VMEM(x.shape, jnp.float32),
+            pltpu.VMEM((n, n), jnp.float32),
             pltpu.VMEM((n, n + 4 * LANES), jnp.float32),
-            pltpu.SemaphoreType.DMA((6,)),
+            pltpu.SemaphoreType.DMA((11,)),
         ],
         compiler_params=pltpu.CompilerParams(vmem_limit_bytes=62 * 2**20),
         name="factor_and_solve",

time: 59.9 us -> 52.1 us (0.87)
  Pallas kernels: 59.1 us -> 51.3 us
    pallas_call x1, Pallas kernels: 17.9 us -> 10.1 us  [factor(): pl.pallas_call(functools.partial(factor_kernel, scale, 2 * SUB, 2), out_s...]
where the time goes in v3:
time: 52.1 us; the launch traced here: 51.9 us
  Pallas kernels  51.3 us (98%)
  between operations  0.64 us (1%)
    pallas_call x1, Pallas kernels, newmark(): pl.pallas_call(functools.partial(newmark_kernel, ndof, nx, ndir), out_sha...  41.1 us
    pallas_call x1, Pallas kernels, factor(): pl.pallas_call(functools.partial(factor_kernel, scale, 2 * SUB, 2), out_s...  10.1 us

profile of v3, /device:TPU:1, one launch (start us, length us, event | category | flops | bytes accessed | tf_op | source)
XLA Modules:
  0.0 51.9 jit_solution(16619272543738012046)
XLA Ops:
  0.6 41.1 %newmark_and_gram.1 = (f32[4,32,1024]{2,1,0:T(8,128)}, f32[4,256,128]{2,1,0:T(8,128)}, f32[3,128,128]{2,1,0:T(8,128)}) custom-call(f32[4,32,1024]{2,1,0:T(8,128)} %disp_in.1, f32[4,32,1024]{2,1,0:T(8,128)} %vel_in.1, f32[8,8,1024]{2,1,0:T(8,128)} %elem_in.1, f32[4,4,1024]{2,1,0:T(4,128)} %link_in.1, f32[4,4,1024]{2,1,0:T(4,128)} %inv_in.1, ...), custom_call_target="tpu_custom_call" | custom-call | tf_op jit(solution)/shard_map/newmark_and_gram/pallas_call | solution.py:455
  41.8 10.1 %factor_and_solve.1 = (f32[4,256,128]{2,1,0:T(8,128)}, f32[256,256]{1,0:T(8,128)}, f32[4,32,1024]{2,1,0:T(8,128)}) custom-call(f32[3,128,128]{2,1,0:T(8,128)} %get-tuple-element.9.gram_in, f32[4,256,128]{2,1,0:T(8,128)} %get-tuple-element.10.x_in, f32[4,32,1024]{2,1,0:T(8,128)} %get-tuple-element.11.vel_in), custom_call_target="tpu_custom_call" | custom-call | tf_op jit(solution)/shard_map/factor_and_solve/pallas_call | solution.py:626

commit v4 on v3

--- a/solution.py
+++ b/solution.py
@@ -46,12 +46,12 @@
     link_in,
     inv_in,
     offset_in,
-    damper_at,
-    damper_k,
-    damper_c,
+    damper_at_in,
+    damper_k_in,
+    damper_c_in,
     vel_out,
     x_out,
-    gram_out,
+    gram,
     disp_a,
     disp_b,
     vel,
@@ -70,7 +70,9 @@
     z_part,
     z_slots,
     z_sum,
-    gram,
+    damper_at,
+    damper_k,
+    damper_c,
     load_sem,
     halo_send,
     halo_recv,
@@ -104,6 +106,9 @@
         (link_in, link_raw),
         (inv_in, inv_raw),
         (offset_in, offset_raw),
+        (damper_at_in, damper_at),
+        (damper_k_in, damper_k),
+        (damper_c_in, damper_c),
     ]
     loads = [pltpu.make_async_copy(s, d, load_sem.at[i]) for i, (s, d) in enumerate(loads)]
     for copy in loads:
@@ -114,12 +119,14 @@
     def greet(p, t):
         pl.semaphore_signal(barrier, inc=1, device_id=(p, t), device_id_type=MESH)
 
+    for by in (1, ndof - 1):
+        greet(lax.rem(me_p + by, ndof), me_t)
+    for by, in far_first([(t,) for t in range(ndir)], (ndir,)):
+        greet(me_p, lax.rem(me_t + by, ndir))
     for by in line:
         greet(lax.rem(me_z + by, nz) * nx + me_x, me_t)
-    for by in (1, ndof - 1):
-        greet(lax.rem(me_p + by, ndof), me_t)
-    for by_x, by_t in plane:
-        greet(me_z * nx + lax.rem(me_x + by_x, nx), lax.rem(me_t + by_t, ndir))
+    for by in range(1, nx):
+        greet(me_z * nx + lax.rem(me_x + by, nx), me_t)
 
     lane = iota((SUB, LANES), 1)
     sub = iota((SUB, LANES), 0)
@@ -127,6 +134,8 @@
     def at_tile(t):
         return pl.ds(pl.multiple_of(t * LANES, LANES), LANES)
 
+    for copy in loads[2:]:
+        copy.wait()
     columns = []
     for q in range(2):
         column = jnp.zeros((SUB, LANES), jnp.float32)
@@ -135,8 +144,6 @@
                 for j in range(2):
                     column = jnp.where(sub == 4 * kind + 2 * i + j, table[i, j, q], column)
         columns.append(column)
-    for copy in loads[2:]:
-        copy.wait()
     for t in range(tiles):
         where = slice(t * LANES, (t + 1) * LANES)
         dense = jnp.zeros((SUB, LANES), jnp.float32)
@@ -169,7 +176,7 @@
                 held = piece if held is None else jnp.where(lane >= REACH * s, piece, held)
             to_send[side, n] = held
 
-    pl.semaphore_wait(barrier, len(line) + 2 + len(plane))
+    pl.semaphore_wait(barrier, 2 + ndir - 1 + nz - 1 + nx - 1)
     halo = []
     for side, by in ((0, 1), (1, ndof - 1)):
         halo.append(
@@ -426,8 +433,6 @@
     own = pltpu.make_async_copy(z_sum.at[:, 0:share, :], gram.at[:, mine, :], ag_recv)
     own.start()
     pltpu.make_async_copy(gram, gram, ag_recv).wait()
-    gram_store = pltpu.make_async_copy(gram, gram_out, store_sem.at[2])
-    gram_store.start()
 
     for copy in halo:
         copy.wait_send()
@@ -440,7 +445,6 @@
         z_copy(by).wait_send()
     vel_store.wait()
     x_store.wait()
-    gram_store.wait()
 
 
 def newmark(ndof, nx, ndir, *args):
@@ -450,17 +454,17 @@
     packs = 2 * (dirs // SUB) + 4
     f32 = jnp.float32
     hbm = pl.BlockSpec(memory_space=pltpu.HBM)
-    smem = pl.BlockSpec(memory_space=pltpu.SMEM)
+    vmem = pl.BlockSpec(memory_space=pltpu.VMEM)
     dma = pltpu.SemaphoreType.DMA
     return pl.pallas_call(
         functools.partial(newmark_kernel, ndof, nx, ndir),
         out_shape=(
-            jax.ShapeDtypeStruct((4, dirs, nodes), f32),
-            jax.ShapeDtypeStruct((4, n, LANES), f32),
-            jax.ShapeDtypeStruct((3, n // 2, n // 2), f32),
+            pltpu.VMEM((4, dirs, nodes), f32),
+            pltpu.VMEM((4, n, LANES), f32),
+            pltpu.VMEM((3, n // 2, n // 2), f32),
         ),
-        in_specs=[hbm] * 6 + [smem] * 3,
-        out_specs=[hbm] * 3,
+        in_specs=[hbm] * 9,
+        out_specs=[vmem] * 3,
         scratch_shapes=[
             pltpu.VMEM((4, dirs, around), f32),
             pltpu.VMEM((4, dirs, around), f32),
@@ -480,8 +484,10 @@
             pltpu.VMEM((3, SUB, n // 2), f32),
             pltpu.VMEM((ndof // nx, 3, SUB, n // 2), f32),
             pltpu.VMEM((3, SUB, n // 2), f32),
-            pltpu.VMEM((3, n // 2, n // 2), f32),
-            dma((6,)),
+            pltpu.SMEM(args[6].shape, jnp.int32),
+            pltpu.SMEM(args[7].shape, f32),
+            pltpu.SMEM(args[8].shape, f32),
+            dma((9,)),
             dma((2,)),
             dma((2,)),
             dma((ndir,)),
@@ -492,13 +498,13 @@
             dma(()),
             dma(()),
             dma(()),
-            dma((3,)),
+            dma((2,)),
         ],
         compiler_params=pltpu.CompilerParams(
-            collective_id=0, has_side_effects=True, vmem_limit_bytes=62 * 2**20
+            collective_id=0, has_side_effects=True, vmem_limit_bytes=32 * 2**20
         ),
         name="newmark_and_gram",
-    )(*args)
+    )(*[pltpu.with_memory_space_constraint(x, pltpu.HBM) for x in args])
 
 
 def spread(x, lane):
@@ -556,28 +562,24 @@
 
 
 def factor_kernel(
-    scale, micro, near, gram_in, x_in, vel_in, q_out, r_out, vel_out, gram, vel, q, r, work, sems
+    scale, micro, near, gram, x, vel, q_out, r_out, vel_out, q, r, work, sems
 ):
     size = gram.shape[1]
     n = 2 * size
-    gram_load = pltpu.make_async_copy(gram_in, gram, sems.at[0])
-    gram_load.start()
+    vel_store = pltpu.make_async_copy(vel, vel_out, sems.at[0])
+    vel_store.start()
     x_loads = [
         pltpu.make_async_copy(
-            x_in.at[c], work.at[:, n + LANES * c : n + LANES * (c + 1)], sems.at[1 + c]
+            x.at[c], work.at[:, n + LANES * c : n + LANES * (c + 1)], sems.at[1 + c]
         )
         for c in range(4)
     ]
     for copy in x_loads:
         copy.start()
-    vel_load = pltpu.make_async_copy(vel_in, vel, sems.at[5])
-    vel_load.start()
-    vel_store = pltpu.make_async_copy(vel, vel_out, sems.at[6])
     stores = []
     row, col = iota((size, size), 0), iota((size, size), 1)
     identity = (row == col).astype(jnp.float32)
     r[size:, 0:size] = jnp.zeros((size, size), jnp.float32)
-    gram_load.wait()
     work[0:size, size:n] = gram[1] * scale
     for low in range(0, n, size):
         high = low + size
@@ -586,8 +588,6 @@
         if low == 0:
             for copy in x_loads:
                 copy.wait()
-            vel_load.wait()
-            vel_store.start()
         later = jnp.dot(
             block[:, size:],
             work[low:high, high:],
@@ -610,8 +610,8 @@
             q[c, low:high, :] = later[:, start : start + LANES]
         part = pl.ds(low, size)
         stores += [
-            pltpu.make_async_copy(q.at[:, part, :], q_out.at[:, part, :], sems.at[7 + low // size]),
-            pltpu.make_async_copy(r.at[part, :], r_out.at[part, :], sems.at[9 + low // size]),
+            pltpu.make_async_copy(q.at[:, part, :], q_out.at[:, part, :], sems.at[5 + low // size]),
+            pltpu.make_async_copy(r.at[part, :], r_out.at[part, :], sems.at[7 + low // size]),
         ]
         for copy in stores[-2:]:
             copy.start()
@@ -622,27 +622,26 @@
 
 def factor(gram, x, vel, scale):
     n = x.shape[1]
+    vmem = pl.BlockSpec(memory_space=pltpu.VMEM)
     hbm = pl.BlockSpec(memory_space=pltpu.HBM)
     return pl.pallas_call(
         functools.partial(factor_kernel, scale, 2 * SUB, 2),
         out_shape=(
-            jax.ShapeDtypeStruct(x.shape, jnp.float32),
-            jax.ShapeDtypeStruct((n, n), jnp.float32),
-            jax.ShapeDtypeStruct(vel.shape, jnp.float32),
+            pltpu.HBM(x.shape, jnp.float32),
+            pltpu.HBM((n, n), jnp.float32),
+            pltpu.HBM(vel.shape, jnp.float32),
         ),
-        in_specs=[hbm, hbm, hbm],
+        in_specs=[vmem, vmem, vmem],
         out_specs=[hbm, hbm, hbm],
         scratch_shapes=[
-            pltpu.VMEM(gram.shape, jnp.float32),
-            pltpu.VMEM(vel.shape, jnp.float32),
             pltpu.VMEM(x.shape, jnp.float32),
             pltpu.VMEM((n, n), jnp.float32),
             pltpu.VMEM((n, n + 4 * LANES), jnp.float32),
-            pltpu.SemaphoreType.DMA((11,)),
+            pltpu.SemaphoreType.DMA((9,)),
         ],
-        compiler_params=pltpu.CompilerParams(vmem_limit_bytes=62 * 2**20),
+        compiler_params=pltpu.CompilerParams(vmem_limit_bytes=32 * 2**20),
         name="factor_and_solve",
-    )(gram, x, vel)
+    )(*[pltpu.with_memory_space_constraint(y, pltpu.VMEM) for y in (gram, x, vel)])
 
 
 def on_device(ndof, ndir, disp, veloc, elem, link, inv, offset, damper_at, damper_k, damper_c):

time: 52.1 us -> 50 us (0.960)
  Pallas kernels: 51.3 us -> 49.2 us
    pallas_call x1, Pallas kernels: 41.1 us -> 40 us  [newmark(): pl.pallas_call(functools.partial(newmark_kernel, ndof, nx, ndir), out_sha...]
    pallas_call x1, Pallas kernels: 10.1 us -> 9.25 us  [factor(): pl.pallas_call(functools.partial(factor_kernel, scale, 2 * SUB, 2), out_s...]
where the time goes in v4:
time: 50 us; the launch traced here: 49.8 us
  Pallas kernels  49.2 us (98%)
  between operations  0.64 us (1%)
    pallas_call x1, Pallas kernels, newmark(): pl.pallas_call(functools.partial(newmark_kernel, ndof, nx, ndir), out_sha...  40 us
    pallas_call x1, Pallas kernels, factor(): pl.pallas_call(functools.partial(factor_kernel, scale, 2 * SUB, 2), out_s...  9.25 us

profile of v4, /device:TPU:1, one launch (start us, length us, event | category | flops | bytes accessed | tf_op | source)
XLA Modules:
  0.0 49.8 jit_solution(4717531269027128315)
XLA Ops:
  0.6 40.0 %newmark_and_gram.1 = (f32[4,32,1024]{2,1,0:T(8,128)S(1)}, f32[4,256,128]{2,1,0:T(8,128)S(1)}, f32[3,128,128]{2,1,0:T(8,128)S(1)}) custom-call(f32[4,32,1024]{2,1,0:T(8,128)} %disp_in.1, f32[4,32,1024]{2,1,0:T(8,128)} %vel_in.1, f32[8,8,1024]{2,1,0:T(8,128)} %elem_in.1, f32[4,4,1024]{2,1,0:T(4,128)} %link_in.1, f32[4,4,1024]{2,1,0:T(4,128)} %inv_in.1, ...), custom_call_target="tpu_custom_call" | custom-call | tf_op jit(solution)/shard_map/newmark_and_gram/pallas_call | solution.py:459
  40.6 9.2 %factor_and_solve.1 = (f32[4,256,128]{2,1,0:T(8,128)}, f32[256,256]{1,0:T(8,128)}, f32[4,32,1024]{2,1,0:T(8,128)}) custom-call(f32[3,128,128]{2,1,0:T(8,128)S(1)} %get-tuple-element.9.gram, f32[4,256,128]{2,1,0:T(8,128)S(1)} %get-tuple-element.10.x, f32[4,32,1024]{2,1,0:T(8,128)S(1)} %get-tuple-element.11.vel), custom_call_target="tpu_custom_call" | custom-call | tf_op jit(solution)/shard_map/factor_and_solve/pallas_call | solution.py:627

commit v5 on v4

--- a/solution.py
+++ b/solution.py
@@ -50,7 +50,7 @@
     damper_k_in,
     damper_c_in,
     vel_out,
-    x_out,
+    x_all,
     gram,
     disp_a,
     disp_b,
@@ -64,7 +64,6 @@
     vm,
     to_send,
     arrived,
-    x_all,
     gram_part,
     slots,
     z_part,
@@ -84,7 +83,6 @@
     z_recv,
     ag_send,
     ag_recv,
-    store_sem,
 ):
     me_p = lax.axis_index("dof")
     me_t = lax.axis_index("dir")
@@ -114,6 +112,8 @@
     for copy in loads:
         copy.start()
 
+    at_x = [lax.rem(me_x + by, nx) for by in range(nx)]
+    at_t = [lax.rem(me_t + by, ndir) for by in range(ndir)]
     barrier = pltpu.get_barrier_semaphore()
 
     def greet(p, t):
@@ -272,7 +272,7 @@
 
     def finish_last(rows, now, acc):
         for i in range(4):
-            vel[i, rows, now] = vel[i, rows, now] + (0.5 * STEP) * acc[i]
+            vel_out[i, rows, now] = vel[i, rows, now] + (0.5 * STEP) * acc[i]
 
     def prepare_tile(t, carry):
         prepare(t)
@@ -282,8 +282,37 @@
         evaluate(disp_a, t, finish_first)
         return carry
 
+    own_rows = pl.ds(pl.multiple_of(me_t * dirs, dirs), dirs)
+
+    def tile_copy(peer, half):
+        part = pl.ds(2 * half, 2)
+        return pltpu.make_async_remote_copy(
+            src_ref=disp_a.at[part, :, at_tile(peer)],
+            dst_ref=x_all.at[part, own_rows, :],
+            send_sem=a2a_send,
+            recv_sem=a2a_recv.at[half],
+            device_id=(me_p, peer),
+            device_id_type=MESH,
+        )
+
+    def send_tile(t, halves):
+        @pl.when(t != me_t)
+        def _():
+            for half in halves:
+                tile_copy(t, half).start()
+
+    def second_tile(t, carry):
+        evaluate(disp_b, t, finish_second)
+        return carry
+
+    def second_and_send(t, carry):
+        evaluate(disp_b, t, finish_second)
+        send_tile(t, (0, 1))
+        return carry
+
     lax.fori_loop(1, tiles, prepare_tile, 0)
     lax.fori_loop(1, tiles - 1, first_tile, 0)
+    lax.fori_loop(2, tiles - 2, second_and_send, 0)
 
     for copy in halo:
         copy.wait_recv()
@@ -303,27 +332,19 @@
     lax.fori_loop(tiles, tiles + 2, lambda k, c: prepare_tile(wrapped(k), c), 0)
     lax.fori_loop(tiles - 1, tiles + 2, lambda k, c: first_tile(wrapped(k), c), 0)
 
-    def tile_copy(peer):
-        return pltpu.make_async_remote_copy(
-            src_ref=disp_a.at[:, :, at_tile(peer)],
-            dst_ref=x_all.at[:, pl.ds(pl.multiple_of(me_t * dirs, dirs), dirs), :],
-            send_sem=a2a_send.at[peer],
-            recv_sem=a2a_recv.at[me_t],
-            device_id=(me_p, peer),
-            device_id_type=MESH,
-        )
-
-    def second_tile(by, carry):
-        t = lax.rem(me_t + by, ndir)
+    def second_then_send(k, carry):
+        t = lax.rem(tiles - 2 + k, tiles)
         evaluate(disp_b, t, finish_second)
-        tile_copy(t).start()
+        send_tile(t, (0,))
         return carry
 
-    half = ndir // 2
-    lax.fori_loop(half, ndir, second_tile, 0)
-    lax.fori_loop(1, half, lambda k, c: second_tile(half - k, c), 0)
-    evaluate(disp_b, me_t, finish_second)
-    x_all[:, pl.ds(pl.multiple_of(me_t * dirs, dirs), dirs), :] = disp_a[:, :, at_tile(me_t)]
+    def send_rest(k, carry):
+        send_tile(lax.rem(tiles - 2 + k, tiles), (1,))
+        return carry
+
+    lax.fori_loop(0, 4, second_then_send, 0)
+    lax.fori_loop(0, 4, send_rest, 0)
+    x_all[:, own_rows, :] = disp_a[:, :, at_tile(me_t)]
     evaluate(disp_b, tiles, finish_second)
 
     def last_tile(t, carry):
@@ -331,43 +352,27 @@
         return carry
 
     lax.fori_loop(0, tiles, last_tile, 0)
-    vel_store = pltpu.make_async_copy(vel.at[:, :, 0:nodes], vel_out, store_sem.at[0])
-    vel_store.start()
-
-    def tile_arrival(by):
-        source = lax.rem(me_t + by, ndir)
-        return pltpu.make_async_remote_copy(
-            src_ref=disp_a.at[:, :, at_tile(source)],
-            dst_ref=x_all.at[:, pl.ds(pl.multiple_of(source * dirs, dirs), dirs), :],
-            send_sem=a2a_send.at[source],
-            recv_sem=a2a_recv.at[source],
-            device_id=(me_p, source),
-            device_id_type=MESH,
-        )
-
-    for by in range(1, ndir):
-        tile_arrival(by).wait_recv()
-    x_store = pltpu.make_async_copy(x_all, x_out, store_sem.at[1])
-    x_store.start()
-
+
+    total = None
+    for half in range(2):
+        arrivals = x_all.at[pl.ds(2 * half, 2), pl.ds(0, (ndir - 1) * dirs), :]
+        pltpu.make_async_copy(arrivals, arrivals, a2a_recv.at[half]).wait()
+        pair = jnp.concatenate([x_all[2 * half], x_all[2 * half + 1]], axis=1)
+        product = lax.dot_general(
+            pair,
+            pair,
+            (((1,), (1,)), ((), ())),
+            precision=HIGHEST,
+            preferred_element_type=jnp.float32,
+        )
+        total = product if total is None else total + product
     half_n = gram.shape[1]
-    halves = [slice(0, half_n), slice(half_n, 2 * half_n)]
-    for b, (i, j) in enumerate(((0, 0), (0, 1), (1, 1))):
-        total = None
-        for c in range(4):
-            product = lax.dot_general(
-                x_all[c, halves[i], :],
-                x_all[c, halves[j], :],
-                (((1,), (1,)), ((), ())),
-                precision=HIGHEST,
-                preferred_element_type=jnp.float32,
-            )
-            total = product if total is None else total + product
-        gram_part[b] = total
+    gram_part[0] = total[0:half_n, 0:half_n]
+    gram_part[1] = total[0:half_n, half_n:]
+    gram_part[2] = total[half_n:, half_n:]
 
     def part_copy(by):
-        peer_x, peer_t = by
-        to = lax.rem(me_x + peer_x, nx), lax.rem(me_t + peer_t, ndir)
+        to = at_x[by[0]], at_t[by[1]]
         member = to[1] * nx + to[0]
         return pltpu.make_async_remote_copy(
             src_ref=gram_part.at[:, pl.ds(member * share, share), :],
@@ -417,8 +422,7 @@
     z_sum[:, 0:share, :] = total
 
     def sum_copy(by):
-        peer_x, peer_t = by
-        to = lax.rem(me_x + peer_x, nx), lax.rem(me_t + peer_t, ndir)
+        to = at_x[by[0]], at_t[by[1]]
         return pltpu.make_async_remote_copy(
             src_ref=z_sum.at[:, 0:share, :],
             dst_ref=gram.at[:, mine, :],
@@ -436,15 +440,13 @@
 
     for copy in halo:
         copy.wait_send()
-    for by in range(1, ndir):
-        tile_copy(lax.rem(me_t + by, ndir)).wait_send()
-    for by in plane:
-        part_copy(by).wait_send()
-        sum_copy(by).wait_send()
-    for by in line:
-        z_copy(by).wait_send()
-    vel_store.wait()
-    x_store.wait()
+    for sent, sem in (
+        (x_all.at[:, 0 : (ndir - 1) * dirs, :], a2a_send),
+        (gram_part.at[:, 0 : len(plane) * share, :], rs_send),
+        (z_slots.at[0 : len(line), :, 0:share, :], z_send),
+        (gram_part.at[:, 0 : len(plane) * share, :], ag_send),
+    ):
+        pltpu.make_async_copy(sent, sent, sem).wait()
 
 
 def newmark(ndof, nx, ndir, *args):
@@ -478,7 +480,6 @@
             pltpu.VMEM((4, SUB, around), f32),
             pltpu.VMEM((2, packs, SUB, LANES), f32),
             pltpu.VMEM((2, packs, SUB, LANES), f32),
-            pltpu.VMEM((4, n, LANES), f32),
             pltpu.VMEM((3, n // 2, n // 2), f32),
             pltpu.VMEM((3, n // 2, n // 2), f32),
             pltpu.VMEM((3, SUB, n // 2), f32),
@@ -490,15 +491,14 @@
             dma((9,)),
             dma((2,)),
             dma((2,)),
-            dma((ndir,)),
-            dma((ndir,)),
+            dma(()),
+            dma((2,)),
             dma(()),
             dma(()),
             dma(()),
             dma(()),
             dma(()),
             dma(()),
-            dma((2,)),
         ],
         compiler_params=pltpu.CompilerParams(
             collective_id=0, has_side_effects=True, vmem_limit_bytes=32 * 2**20

time: 50 us -> 49.7 us (level)
  no operation moved by 1% of the time
where the time goes in v5:
time: 49.7 us; the launch traced here: 49.6 us
  Pallas kernels  48.9 us (98%)
  between operations  0.64 us (1%)
    pallas_call x1, Pallas kernels, newmark(): pl.pallas_call(functools.partial(newmark_kernel, ndof, nx, ndir), out_sha...  39.7 us
    pallas_call x1, Pallas kernels, factor(): pl.pallas_call(functools.partial(factor_kernel, scale, 2 * SUB, 2), out_s...  9.25 us

profile of v5, /device:TPU:1, one launch (start us, length us, event | category | flops | bytes accessed | tf_op | source)
XLA Modules:
  0.0 49.6 jit_solution(8413841598959093045)
XLA Ops:
  0.6 39.7 %newmark_and_gram.1 = (f32[4,32,1024]{2,1,0:T(8,128)S(1)}, f32[4,256,128]{2,1,0:T(8,128)S(1)}, f32[3,128,128]{2,1,0:T(8,128)S(1)}) custom-call(f32[4,32,1024]{2,1,0:T(8,128)} %disp_in.1, f32[4,32,1024]{2,1,0:T(8,128)} %vel_in.1, f32[8,8,1024]{2,1,0:T(8,128)} %elem_in.1, f32[4,4,1024]{2,1,0:T(4,128)} %link_in.1, f32[4,4,1024]{2,1,0:T(4,128)} %inv_in.1, ...), custom_call_target="tpu_custom_call" | custom-call | tf_op jit(solution)/shard_map/newmark_and_gram/pallas_call | solution.py:461
  40.3 9.2 %factor_and_solve.1 = (f32[4,256,128]{2,1,0:T(8,128)}, f32[256,256]{1,0:T(8,128)}, f32[4,32,1024]{2,1,0:T(8,128)}) custom-call(f32[3,128,128]{2,1,0:T(8,128)S(1)} %get-tuple-element.9.gram, f32[4,256,128]{2,1,0:T(8,128)S(1)} %get-tuple-element.10.x, f32[4,32,1024]{2,1,0:T(8,128)S(1)} %get-tuple-element.11.vel), custom_call_target="tpu_custom_call" | custom-call | tf_op jit(solution)/shard_map/factor_and_solve/pallas_call | solution.py:627

commit v6 on v5

--- a/solution.py
+++ b/solution.py
@@ -97,6 +97,15 @@
     plane = far_first([(x, t) for x in range(nx) for t in range(ndir)], (nx, ndir))
     line = [by for by, in far_first([(z,) for z in range(nz)], (nz,))]
 
+    at_x = [lax.rem(me_x + by, nx) for by in range(nx)]
+    at_t = [lax.rem(me_t + by, ndir) for by in range(ndir)]
+    barrier = pltpu.get_barrier_semaphore()
+
+    def greet(p, t):
+        pl.semaphore_signal(barrier, inc=1, device_id=(p, t), device_id_type=MESH)
+
+    for by in (1, ndof - 1):
+        greet(lax.rem(me_p + by, ndof), me_t)
     loads = [
         (disp_in, disp_a.at[:, :, 0:nodes]),
         (vel_in, vel.at[:, :, 0:nodes]),
@@ -112,15 +121,6 @@
     for copy in loads:
         copy.start()
 
-    at_x = [lax.rem(me_x + by, nx) for by in range(nx)]
-    at_t = [lax.rem(me_t + by, ndir) for by in range(ndir)]
-    barrier = pltpu.get_barrier_semaphore()
-
-    def greet(p, t):
-        pl.semaphore_signal(barrier, inc=1, device_id=(p, t), device_id_type=MESH)
-
-    for by in (1, ndof - 1):
-        greet(lax.rem(me_p + by, ndof), me_t)
     for by, in far_first([(t,) for t in range(ndir)], (ndir,)):
         greet(me_p, lax.rem(me_t + by, ndir))
     for by in line:
@@ -330,20 +330,25 @@
         return lax.rem(k, around)
 
     lax.fori_loop(tiles, tiles + 2, lambda k, c: prepare_tile(wrapped(k), c), 0)
-    lax.fori_loop(tiles - 1, tiles + 2, lambda k, c: first_tile(wrapped(k), c), 0)
-
-    def second_then_send(k, carry):
-        t = lax.rem(tiles - 2 + k, tiles)
+
+    def inner_end(k, carry):
+        evaluate(disp_a, lax.rem(tiles - 1 + k, tiles), finish_first)
+        return second_and_send(lax.rem(tiles - 2 + 3 * k, tiles), carry)
+
+    def outer_end(k, carry):
+        t = lax.rem(tiles - 1 + k, tiles)
         evaluate(disp_b, t, finish_second)
         send_tile(t, (0,))
         return carry
 
     def send_rest(k, carry):
-        send_tile(lax.rem(tiles - 2 + k, tiles), (1,))
+        send_tile(lax.rem(tiles - 1 + k, tiles), (1,))
         return carry
 
-    lax.fori_loop(0, 4, second_then_send, 0)
-    lax.fori_loop(0, 4, send_rest, 0)
+    lax.fori_loop(0, 2, inner_end, 0)
+    lax.fori_loop(tiles, tiles + 1, first_tile, 0)
+    lax.fori_loop(0, 2, outer_end, 0)
+    lax.fori_loop(0, 2, send_rest, 0)
     x_all[:, own_rows, :] = disp_a[:, :, at_tile(me_t)]
     evaluate(disp_b, tiles, finish_second)
 
@@ -517,35 +522,51 @@
 
 def eliminate(block, micro, near):
     size, width = block.shape
-    row = iota((micro, LANES), 0)
+    sub = iota((SUB, LANES), 0)
+    groups = micro // SUB
     rows = [block[i : i + SUB] for i in range(0, size, SUB)]
     done = []
     for s in range(0, size, micro):
-        top = jnp.concatenate(rows[: micro // SUB], axis=0)
-        rest = rows[micro // SUB :]
-        column = [spread(top, s + j) for j in range(micro)]
+        top = rows[:groups]
+        rest = rows[groups:]
+        column = [
+            [spread(top[g], s + j) if g >= j // SUB else None for g in range(groups)]
+            for j in range(micro)
+        ]
+
+        def entry(j, m):
+            return column[j][m // SUB][m % SUB : m % SUB + 1]
+
         inverse = []
-        pivots = jnp.broadcast_to(column[0][0:1], (micro, LANES))
+        pivots = [None] * groups
         for j in range(micro):
-            pivot = column[j][j : j + 1]
+            group, at = j // SUB, j % SUB
+            pivot = entry(j, j)
             inverse.append(1.0 / pivot)
-            pivots = jnp.where(row == j, pivot, pivots)
-            if j == micro - 1:
-                break
-            factor = jnp.where(row > j, column[j] * inverse[j], 0.0)
-            for m in range(j + 1, micro):
-                column[m] = column[m] - factor * column[m][j : j + 1]
-            top = top - tiled(factor, width) * top[j : j + 1]
+            held = jnp.broadcast_to(pivot, (SUB, LANES))
+            pivots[group] = held if at == 0 else jnp.where(sub == at, held, pivots[group])
+            source = top[group][at : at + 1]
+            for g in range(group, groups):
+                if g == group and at == SUB - 1:
+                    continue
+                factor = column[j][g] * inverse[j]
+                if g == group:
+                    factor = jnp.where(sub > at, factor, 0.0)
+                for m in range(j + 1, min(micro, (g + 1) * SUB)):
+                    column[m][g] = column[m][g] - factor * entry(j, m)
+                top[g] = top[g] - tiled(factor, width) * source
         rows = []
         for part in rest[:near]:
             own = [spread(part, s + j) for j in range(micro)]
             for j in range(micro):
                 factor = own[j] * inverse[j]
                 for m in range(j + 1, micro):
-                    own[m] = own[m] - factor * column[m][j : j + 1]
-                part = part - tiled(factor, width) * top[j : j + 1]
+                    own[m] = own[m] - factor * entry(j, m)
+                part = part - tiled(factor, width) * top[j // SUB][j % SUB : j % SUB + 1]
             rows.append(part)
-        top = top * tiled(lax.rsqrt(pivots), width)
+        top = jnp.concatenate(
+            [t * tiled(lax.rsqrt(p), width) for t, p in zip(top, pivots)], axis=0
+        )
         if len(rest) > near:
             update = lax.dot_general(
                 top[:, 0:size],

time: 49.7 us -> 48.2 us (0.970)
  Pallas kernels: 48.9 us -> 47.4 us
    pallas_call x1, Pallas kernels: 9.25 us -> 8.43 us  [factor(): pl.pallas_call(functools.partial(factor_kernel, scale, 2 * SUB, 2), out_s...]
    pallas_call x1, Pallas kernels: 39.7 us -> 39 us  [newmark(): pl.pallas_call(functools.partial(newmark_kernel, ndof, nx, ndir), out_sha...]
where the time goes in v6:
time: 48.2 us; the launch traced here: 48.1 us
  Pallas kernels  47.4 us (98%)
  between operations  0.64 us (1%)
    pallas_call x1, Pallas kernels, newmark(): pl.pallas_call(functools.partial(newmark_kernel, ndof, nx, ndir), out_sha...  39 us
    pallas_call x1, Pallas kernels, factor(): pl.pallas_call(functools.partial(factor_kernel, scale, 2 * SUB, 2), out_s...  8.43 us

profile of v6, /device:TPU:1, one launch (start us, length us, event | category | flops | bytes accessed | tf_op | source)
XLA Modules:
  0.0 48.1 jit_solution(10021904148452371096)
XLA Ops:
  0.6 39.0 %newmark_and_gram.1 = (f32[4,32,1024]{2,1,0:T(8,128)S(1)}, f32[4,256,128]{2,1,0:T(8,128)S(1)}, f32[3,128,128]{2,1,0:T(8,128)S(1)}) custom-call(f32[4,32,1024]{2,1,0:T(8,128)} %disp_in.1, f32[4,32,1024]{2,1,0:T(8,128)} %vel_in.1, f32[8,8,1024]{2,1,0:T(8,128)} %elem_in.1, f32[4,4,1024]{2,1,0:T(4,128)} %link_in.1, f32[4,4,1024]{2,1,0:T(4,128)} %inv_in.1, ...), custom_call_target="tpu_custom_call" | custom-call | tf_op jit(solution)/shard_map/newmark_and_gram/pallas_call | solution.py:466
  39.6 8.4 %factor_and_solve.1 = (f32[4,256,128]{2,1,0:T(8,128)}, f32[256,256]{1,0:T(8,128)}, f32[4,32,1024]{2,1,0:T(8,128)}) custom-call(f32[3,128,128]{2,1,0:T(8,128)S(1)} %get-tuple-element.9.gram, f32[4,256,128]{2,1,0:T(8,128)S(1)} %get-tuple-element.10.x, f32[4,32,1024]{2,1,0:T(8,128)S(1)} %get-tuple-element.11.vel), custom_call_target="tpu_custom_call" | custom-call | tf_op jit(solution)/shard_map/factor_and_solve/pallas_call | solution.py:648

commit v7 on v6

--- a/solution.py
+++ b/solution.py
@@ -589,53 +589,45 @@
     n = 2 * size
     vel_store = pltpu.make_async_copy(vel, vel_out, sems.at[0])
     vel_store.start()
-    x_loads = [
-        pltpu.make_async_copy(
-            x.at[c], work.at[:, n + LANES * c : n + LANES * (c + 1)], sems.at[1 + c]
-        )
-        for c in range(4)
-    ]
-    for copy in x_loads:
+    stores = []
+
+    def store(source, target):
+        copy = pltpu.make_async_copy(source, target, sems.at[1 + len(stores)])
         copy.start()
-    stores = []
+        stores.append(copy)
+
+    def product(left, right, dims=(((1,), (0,)), ((), ()))):
+        return lax.dot_general(
+            left, right, dims, precision=HIGHEST, preferred_element_type=jnp.float32
+        )
+
+    transposed = (((0,), (0,)), ((), ()))
     row, col = iota((size, size), 0), iota((size, size), 1)
     identity = (row == col).astype(jnp.float32)
+    upper, lower = pl.ds(0, size), pl.ds(size, size)
     r[size:, 0:size] = jnp.zeros((size, size), jnp.float32)
-    work[0:size, size:n] = gram[1] * scale
-    for low in range(0, n, size):
-        high = low + size
-        block = gram[0] * scale if low == 0 else work[low:high, low:high]
-        block = eliminate(jnp.concatenate([block, identity], axis=1), micro, near)
-        if low == 0:
-            for copy in x_loads:
-                copy.wait()
-        later = jnp.dot(
-            block[:, size:],
-            work[low:high, high:],
-            precision=HIGHEST,
-            preferred_element_type=jnp.float32,
-        )
-        r[low:high, low:high] = jnp.where(row <= col, block[:, 0:size], 0.0)
-        if low == 0:
-            r[low:high, high:n] = later[:, 0:size]
-            work[high:, high:n] = gram[2] * scale
-            work[high:, high:] = work[high:, high:] - lax.dot_general(
-                later[:, 0:size],
-                later,
-                (((0,), (0,)), ((), ())),
-                precision=HIGHEST,
-                preferred_element_type=jnp.float32,
-            )
-        for c in range(4):
-            start = n - high + LANES * c
-            q[c, low:high, :] = later[:, start : start + LANES]
-        part = pl.ds(low, size)
-        stores += [
-            pltpu.make_async_copy(q.at[:, part, :], q_out.at[:, part, :], sems.at[5 + low // size]),
-            pltpu.make_async_copy(r.at[part, :], r_out.at[part, :], sems.at[7 + low // size]),
-        ]
-        for copy in stores[-2:]:
-            copy.start()
+
+    block = eliminate(jnp.concatenate([gram[0] * scale, identity], axis=1), micro, near)
+    inverse = block[:, size:]
+    side = product(inverse, gram[1] * scale)
+    corner = gram[2] * scale - product(side, side, transposed)
+    r[0:size, 0:size] = jnp.where(row <= col, block[:, 0:size], 0.0)
+    r[0:size, size:n] = side
+    for c in range(4):
+        first = product(inverse, x[c, 0:size, :])
+        q[c, 0:size, :] = first
+        work[c] = x[c, size:n, :] - product(side, first, transposed)
+
+    block = eliminate(jnp.concatenate([corner, identity], axis=1), micro, near)
+    inverse = block[:, size:]
+    store(r.at[upper, :], r_out.at[upper, :])
+    for c in range(4):
+        store(q.at[c, upper, :], q_out.at[c, upper, :])
+    r[size:n, size:n] = jnp.where(row <= col, block[:, 0:size], 0.0)
+    store(r.at[lower, :], r_out.at[lower, :])
+    for c in range(4):
+        q[c, size:n, :] = product(inverse, work[c])
+        store(q.at[c, lower, :], q_out.at[c, lower, :])
     for copy in stores:
         copy.wait()
     vel_store.wait()
@@ -657,8 +649,8 @@
         scratch_shapes=[
             pltpu.VMEM(x.shape, jnp.float32),
             pltpu.VMEM((n, n), jnp.float32),
-            pltpu.VMEM((n, n + 4 * LANES), jnp.float32),
-            pltpu.SemaphoreType.DMA((9,)),
+            pltpu.VMEM((4, n // 2, LANES), jnp.float32),
+            pltpu.SemaphoreType.DMA((11,)),
         ],
         compiler_params=pltpu.CompilerParams(vmem_limit_bytes=32 * 2**20),
         name="factor_and_solve",

time: 48.2 us -> 47.9 us (level)
  no operation moved by 1% of the time
where the time goes in v7:
time: 47.9 us; the launch traced here: 47.8 us
  Pallas kernels  47.1 us (98%)
  between operations  0.64 us (1%)
    pallas_call x1, Pallas kernels, newmark(): pl.pallas_call(functools.partial(newmark_kernel, ndof, nx, ndir), out_sha...  39 us
    pallas_call x1, Pallas kernels, factor(): pl.pallas_call(functools.partial(factor_kernel, scale, 2 * SUB, 2), out_s...  8.13 us

profile of v7, /device:TPU:1, one launch (start us, length us, event | category | flops | bytes accessed | tf_op | source)
XLA Modules:
  0.0 47.8 jit_solution(616121827927263581)
XLA Ops:
  0.6 39.0 %newmark_and_gram.1 = (f32[4,32,1024]{2,1,0:T(8,128)S(1)}, f32[4,256,128]{2,1,0:T(8,128)S(1)}, f32[3,128,128]{2,1,0:T(8,128)S(1)}) custom-call(f32[4,32,1024]{2,1,0:T(8,128)} %disp_in.1, f32[4,32,1024]{2,1,0:T(8,128)} %vel_in.1, f32[8,8,1024]{2,1,0:T(8,128)} %elem_in.1, f32[4,4,1024]{2,1,0:T(4,128)} %link_in.1, f32[4,4,1024]{2,1,0:T(4,128)} %inv_in.1, ...), custom_call_target="tpu_custom_call" | custom-call | tf_op jit(solution)/shard_map/newmark_and_gram/pallas_call | solution.py:466
  39.6 8.1 %factor_and_solve.1 = (f32[4,256,128]{2,1,0:T(8,128)}, f32[256,256]{1,0:T(8,128)}, f32[4,32,1024]{2,1,0:T(8,128)}) custom-call(f32[3,128,128]{2,1,0:T(8,128)S(1)} %get-tuple-element.9.gram, f32[4,256,128]{2,1,0:T(8,128)S(1)} %get-tuple-element.10.x, f32[4,32,1024]{2,1,0:T(8,128)S(1)} %get-tuple-element.11.vel), custom_call_target="tpu_custom_call" | custom-call | tf_op jit(solution)/shard_map/factor_and_solve/pallas_call | solution.py:640

commit v8 on v7

--- a/solution.py
+++ b/solution.py
@@ -312,7 +312,7 @@
 
     lax.fori_loop(1, tiles, prepare_tile, 0)
     lax.fori_loop(1, tiles - 1, first_tile, 0)
-    lax.fori_loop(2, tiles - 2, second_and_send, 0)
+    lax.fori_loop(0, 2, lambda k, c: second_and_send(2 + (tiles - 5) * k, c), 0)
 
     for copy in halo:
         copy.wait_recv()
@@ -333,7 +333,8 @@
 
     def inner_end(k, carry):
         evaluate(disp_a, lax.rem(tiles - 1 + k, tiles), finish_first)
-        return second_and_send(lax.rem(tiles - 2 + 3 * k, tiles), carry)
+        second_and_send(lax.rem(tiles - 2 + 3 * k, tiles), carry)
+        return second_and_send(3 + k, carry)
 
     def outer_end(k, carry):
         t = lax.rem(tiles - 1 + k, tiles)

time: 47.9 us -> 48.5 us (1.013)
  Pallas kernels: 47.1 us -> 47.8 us
    pallas_call x1, Pallas kernels: 39 us -> 39.6 us  [newmark(): pl.pallas_call(functools.partial(newmark_kernel, ndof, nx, ndir), out_sha...]
where the time goes in v8:
time: 48.5 us; the launch traced here: 48.4 us
  Pallas kernels  47.8 us (99%)
  between operations  0.64 us (1%)
    pallas_call x1, Pallas kernels, newmark(): pl.pallas_call(functools.partial(newmark_kernel, ndof, nx, ndir), out_sha...  39.6 us
    pallas_call x1, Pallas kernels, factor(): pl.pallas_call(functools.partial(factor_kernel, scale, 2 * SUB, 2), out_s...  8.13 us

profile of v8, /device:TPU:1, one launch (start us, length us, event | category | flops | bytes accessed | tf_op | source)
XLA Modules:
  0.0 48.4 jit_solution(7779856247479579173)
XLA Ops:
  0.6 39.6 %newmark_and_gram.1 = (f32[4,32,1024]{2,1,0:T(8,128)S(1)}, f32[4,256,128]{2,1,0:T(8,128)S(1)}, f32[3,128,128]{2,1,0:T(8,128)S(1)}) custom-call(f32[4,32,1024]{2,1,0:T(8,128)} %disp_in.1, f32[4,32,1024]{2,1,0:T(8,128)} %vel_in.1, f32[8,8,1024]{2,1,0:T(8,128)} %elem_in.1, f32[4,4,1024]{2,1,0:T(4,128)} %link_in.1, f32[4,4,1024]{2,1,0:T(4,128)} %inv_in.1, ...), custom_call_target="tpu_custom_call" | custom-call | tf_op jit(solution)/shard_map/newmark_and_gram/pallas_call | solution.py:467
  40.3 8.1 %factor_and_solve.1 = (f32[4,256,128]{2,1,0:T(8,128)}, f32[256,256]{1,0:T(8,128)}, f32[4,32,1024]{2,1,0:T(8,128)}) custom-call(f32[3,128,128]{2,1,0:T(8,128)S(1)} %get-tuple-element.9.gram, f32[4,256,128]{2,1,0:T(8,128)S(1)} %get-tuple-element.10.x, f32[4,32,1024]{2,1,0:T(8,128)S(1)} %get-tuple-element.11.vel), custom_call_target="tpu_custom_call" | custom-call | tf_op jit(solution)/shard_map/factor_and_solve/pallas_call | solution.py:641

commit v9 on v7

--- a/solution.py
+++ b/solution.py
@@ -310,9 +310,17 @@
         send_tile(t, (0, 1))
         return carry
 
-    lax.fori_loop(1, tiles, prepare_tile, 0)
-    lax.fori_loop(1, tiles - 1, first_tile, 0)
-    lax.fori_loop(2, tiles - 2, second_and_send, 0)
+    def prepare_and_first(t, carry):
+        prepare(t)
+        return first_tile(t, carry)
+
+    def advance(t, carry):
+        prepare_and_first(t + 1, carry)
+        return second_and_send(t, carry)
+
+    lax.fori_loop(1, 3, prepare_and_first, 0)
+    lax.fori_loop(2, tiles - 2, advance, 0)
+    prepare(tiles - 1)
 
     for copy in halo:
         copy.wait_recv()

time: 47.9 us -> 49.1 us (1.025)
  Pallas kernels: 47.1 us -> 48.3 us
    pallas_call x1, Pallas kernels: 39 us -> 40.2 us  [newmark(): pl.pallas_call(functools.partial(newmark_kernel, ndof, nx, ndir), out_sha...]
where the time goes in v9:
time: 49.1 us; the launch traced here: 49 us
  Pallas kernels  48.3 us (98%)
  between operations  0.64 us (1%)
    pallas_call x1, Pallas kernels, newmark(): pl.pallas_call(functools.partial(newmark_kernel, ndof, nx, ndir), out_sha...  40.2 us
    pallas_call x1, Pallas kernels, factor(): pl.pallas_call(functools.partial(factor_kernel, scale, 2 * SUB, 2), out_s...  8.13 us

profile of v9, /device:TPU:1, one launch (start us, length us, event | category | flops | bytes accessed | tf_op | source)
XLA Modules:
  0.0 49.0 jit_solution(5861918931934213967)
XLA Ops:
  0.6 40.2 %newmark_and_gram.1 = (f32[4,32,1024]{2,1,0:T(8,128)S(1)}, f32[4,256,128]{2,1,0:T(8,128)S(1)}, f32[3,128,128]{2,1,0:T(8,128)S(1)}) custom-call(f32[4,32,1024]{2,1,0:T(8,128)} %disp_in.1, f32[4,32,1024]{2,1,0:T(8,128)} %vel_in.1, f32[8,8,1024]{2,1,0:T(8,128)} %elem_in.1, f32[4,4,1024]{2,1,0:T(4,128)} %link_in.1, f32[4,4,1024]{2,1,0:T(4,128)} %inv_in.1, ...), custom_call_target="tpu_custom_call" | custom-call | tf_op jit(solution)/shard_map/newmark_and_gram/pallas_call | solution.py:474
  40.8 8.1 %factor_and_solve.1 = (f32[4,256,128]{2,1,0:T(8,128)}, f32[256,256]{1,0:T(8,128)}, f32[4,32,1024]{2,1,0:T(8,128)}) custom-call(f32[3,128,128]{2,1,0:T(8,128)S(1)} %get-tuple-element.9.gram, f32[4,256,128]{2,1,0:T(8,128)S(1)} %get-tuple-element.10.x, f32[4,32,1024]{2,1,0:T(8,128)S(1)} %get-tuple-element.11.vel), custom_call_target="tpu_custom_call" | custom-call | tf_op jit(solution)/shard_map/factor_and_solve/pallas_call | solution.py:648

commit v10 on v7

--- a/solution.py
+++ b/solution.py
@@ -350,13 +350,10 @@
     lax.fori_loop(0, 2, outer_end, 0)
     lax.fori_loop(0, 2, send_rest, 0)
     x_all[:, own_rows, :] = disp_a[:, :, at_tile(me_t)]
-    evaluate(disp_b, tiles, finish_second)
 
     def last_tile(t, carry):
         evaluate(disp_a, t, finish_last)
         return carry
-
-    lax.fori_loop(0, tiles, last_tile, 0)
 
     total = None
     for half in range(2):
@@ -393,6 +390,8 @@
     mine = pl.ds(me * share, share)
     own = pltpu.make_async_copy(gram_part.at[:, mine, :], slots.at[:, mine, :], rs_recv)
     own.start()
+    evaluate(disp_b, tiles, finish_second)
+    lax.fori_loop(0, tiles, last_tile, 0)
     pltpu.make_async_copy(slots, slots, rs_recv).wait()
     total = slots[:, 0:SUB, :]
     for k in range(SUB, slots.shape[1], SUB):

time: 47.9 us -> 47.9 us (level)
  no operation moved by 1% of the time
where the time goes in v10:
time: 47.9 us; the launch traced here: 47.8 us
  Pallas kernels  47.2 us (99%)
  between operations  0.64 us (1%)
    pallas_call x1, Pallas kernels, newmark(): pl.pallas_call(functools.partial(newmark_kernel, ndof, nx, ndir), out_sha...  39 us
    pallas_call x1, Pallas kernels, factor(): pl.pallas_call(functools.partial(factor_kernel, scale, 2 * SUB, 2), out_s...  8.13 us

profile of v10, /device:TPU:1, one launch (start us, length us, event | category | flops | bytes accessed | tf_op | source)
XLA Modules:
  0.0 47.8 jit_solution(8329166592812093970)
XLA Ops:
  0.6 39.0 %newmark_and_gram.1 = (f32[4,32,1024]{2,1,0:T(8,128)S(1)}, f32[4,256,128]{2,1,0:T(8,128)S(1)}, f32[3,128,128]{2,1,0:T(8,128)S(1)}) custom-call(f32[4,32,1024]{2,1,0:T(8,128)} %disp_in.1, f32[4,32,1024]{2,1,0:T(8,128)} %vel_in.1, f32[8,8,1024]{2,1,0:T(8,128)} %elem_in.1, f32[4,4,1024]{2,1,0:T(4,128)} %link_in.1, f32[4,4,1024]{2,1,0:T(4,128)} %inv_in.1, ...), custom_call_target="tpu_custom_call" | custom-call | tf_op jit(solution)/shard_map/newmark_and_gram/pallas_call | solution.py:465
  39.7 8.1 %factor_and_solve.1 = (f32[4,256,128]{2,1,0:T(8,128)}, f32[256,256]{1,0:T(8,128)}, f32[4,32,1024]{2,1,0:T(8,128)}) custom-call(f32[3,128,128]{2,1,0:T(8,128)S(1)} %get-tuple-element.9.gram, f32[4,256,128]{2,1,0:T(8,128)S(1)} %get-tuple-element.10.x, f32[4,32,1024]{2,1,0:T(8,128)S(1)} %get-tuple-element.11.vel), custom_call_target="tpu_custom_call" | custom-call | tf_op jit(solution)/shard_map/factor_and_solve/pallas_call | solution.py:639

commit v11 on v7

--- a/solution.py
+++ b/solution.py
@@ -338,17 +338,12 @@
     def outer_end(k, carry):
         t = lax.rem(tiles - 1 + k, tiles)
         evaluate(disp_b, t, finish_second)
-        send_tile(t, (0,))
-        return carry
-
-    def send_rest(k, carry):
-        send_tile(lax.rem(tiles - 1 + k, tiles), (1,))
+        send_tile(t, (0, 1))
         return carry
 
     lax.fori_loop(0, 2, inner_end, 0)
     lax.fori_loop(tiles, tiles + 1, first_tile, 0)
     lax.fori_loop(0, 2, outer_end, 0)
-    lax.fori_loop(0, 2, send_rest, 0)
     x_all[:, own_rows, :] = disp_a[:, :, at_tile(me_t)]
     evaluate(disp_b, tiles, finish_second)
 

time: 47.9 us -> 47.9 us (level)
  no operation moved by 1% of the time
where the time goes in v11:
time: 47.9 us; the launch traced here: 47.8 us
  Pallas kernels  47.1 us (98%)
  between operations  0.64 us (1%)
    pallas_call x1, Pallas kernels, newmark(): pl.pallas_call(functools.partial(newmark_kernel, ndof, nx, ndir), out_sha...  39 us
    pallas_call x1, Pallas kernels, factor(): pl.pallas_call(functools.partial(factor_kernel, scale, 2 * SUB, 2), out_s...  8.13 us

profile of v11, /device:TPU:1, one launch (start us, length us, event | category | flops | bytes accessed | tf_op | source)
XLA Modules:
  0.0 47.8 jit_solution(9684846914023358127)
XLA Ops:
  0.6 39.0 %newmark_and_gram.1 = (f32[4,32,1024]{2,1,0:T(8,128)S(1)}, f32[4,256,128]{2,1,0:T(8,128)S(1)}, f32[3,128,128]{2,1,0:T(8,128)S(1)}) custom-call(f32[4,32,1024]{2,1,0:T(8,128)} %disp_in.1, f32[4,32,1024]{2,1,0:T(8,128)} %vel_in.1, f32[8,8,1024]{2,1,0:T(8,128)} %elem_in.1, f32[4,4,1024]{2,1,0:T(4,128)} %link_in.1, f32[4,4,1024]{2,1,0:T(4,128)} %inv_in.1, ...), custom_call_target="tpu_custom_call" | custom-call | tf_op jit(solution)/shard_map/newmark_and_gram/pallas_call | solution.py:461
  39.6 8.1 %factor_and_solve.1 = (f32[4,256,128]{2,1,0:T(8,128)}, f32[256,256]{1,0:T(8,128)}, f32[4,32,1024]{2,1,0:T(8,128)}) custom-call(f32[3,128,128]{2,1,0:T(8,128)S(1)} %get-tuple-element.9.gram, f32[4,256,128]{2,1,0:T(8,128)S(1)} %get-tuple-element.10.x, f32[4,32,1024]{2,1,0:T(8,128)S(1)} %get-tuple-element.11.vel), custom_call_target="tpu_custom_call" | custom-call | tf_op jit(solution)/shard_map/factor_and_solve/pallas_call | solution.py:635
